TPU v7x, 128 devices: a whole 4x4x4 slice. The times are simulated.
128 devices in a mesh: chan: 32 (over z_lo, x, y), hour: 4 (over z_hi, core).
Axes of the slice: x: 4, y: 4, z: 4 (z_hi: 2, z_lo: 2; z = z_hi * 2 + z_lo), core: 2. Of those that a mesh axis runs over, the one named last changes fastest.
Arguments:
- samples: bfloat16 [128, 1024, 1024], P('hour', 'chan'), may hold values from -400 to 400, as said below
- gap_starts: int32 [128, 4], P('hour'), may hold values from 0 to 1023
- valid_counts: int32 [128], P('hour'), may hold values from 512 to 1024
- owners: int32 [128, 1], P('hour'), may hold values from 0 to 7
- pair_mask: int32 [1024, 17, 32], P('chan'), may hold values 0 or 1
Outputs:
- xstack: bfloat16 [1024, 17, 32, 2, 512], P('chan', None, None, None, 'hour')
Inputs may be any that keep to these rules, and one draw needn't show every extreme that they name: `owners`: every owner group of the window owns at least one segment. `samples`: products of a channel gain, a slowly varying envelope and noise with a part common to all channels.
All inputs are finite; a program needn't handle non-finite values. No bound on the sum of `pair_mask` on one device may be relied on, other than what follows from the above.
Results may differ from a plain program's by a relative error of at most 0.0035.
Values may be sent and summed in bfloat16 or wider, within the bound.
No kernel may reach another device: no remote copies, remote signals or barrier semaphores. Data moves between devices by JAX's collectives and lax.ppermute only.
A program may use at most 192 MiB of HBM per device.

v0:
```python
import functools
import math

import jax
import jax.numpy as jnp
import ml_dtypes
import numpy as np
from jax import lax
from jax.experimental import pallas as pl
from jax.experimental.pallas import tpu as pltpu
from jax.sharding import Mesh, PartitionSpec as P

L = 1024
HGROUPS = 8
BINS = 512
GAPW = 32
RAMW = 64
SMW = 64
NF = 8
PARTS = 4
MB = 1024 * 1024


def band_np(length, half_width):
    places = np.arange(length)
    return (np.abs(places[:, None] - places[None, :]) <= half_width).astype(ml_dtypes.bfloat16)


def inverse_count_np(length, half_width):
    places = np.arange(length)
    upper = np.minimum(places + half_width, length - 1)
    lower = np.maximum(places - half_width, 0)
    return (1.0 / (upper - lower + 1)).astype(np.float32)


def dft_rows_np():
    phase = np.arange(BINS)[:, None] * np.arange(L)[None, :] % L
    angle = 2.0 * math.pi / L * phase
    return np.concatenate([np.cos(angle), -np.sin(angle)], axis=0).astype(ml_dtypes.bfloat16)


def taper_np():
    return (0.5 - 0.5 * np.cos(2.0 * math.pi / L * np.arange(L))).astype(np.float32)


def spread_np():
    table = np.zeros((256, 512), np.float32)
    c = np.arange(128)
    table[c, 2 * c] = 1
    table[128 + c, 2 * c + 1] = -1
    table[128 + c, 256 + 2 * c] = 1
    table[c, 256 + 2 * c + 1] = 1
    return table.astype(ml_dtypes.bfloat16)


def cost(us):
    return pl.CostEstimate(flops=int(us * 3.45e+10), bytes_accessed=int(us * 1.08e+08), transcendentals=0)


def dot(a, b, contract=((1,), (0,))):
    return lax.dot_general(a, b, (contract, ((), ())), preferred_element_type=jnp.float32)


def lanes(shape):
    return lax.broadcasted_iota(jnp.int32, shape, len(shape) - 1)


WROWS = 512


def level_kernel(x_ref, valid_ref, band_ref, taper_ref, icount_ref, out_ref):
    x = x_ref[...].astype(jnp.float32).reshape(WROWS // 32, 32, L) * valid_ref[...][:, None, :]
    x = x.reshape(WROWS, L)
    level = dot(jnp.abs(x).astype(jnp.bfloat16), band_ref[...]) * icount_ref[...]
    out_ref[...] = (taper_ref[...] * x / (level + 1e-06)).astype(jnp.bfloat16)


def whole(*shape):
    return pl.BlockSpec(shape, lambda *i: (0,) * len(shape))


def normalize(rows, valid):
    return pl.pallas_call(
        level_kernel,
        grid=(1024 // WROWS,),
        in_specs=[
            pl.BlockSpec((WROWS, L), lambda i: (i, 0)),
            pl.BlockSpec((WROWS // 32, L), lambda i: (i, 0)),
            whole(L, L),
            whole(1, L),
            whole(1, L),
        ],
        out_specs=pl.BlockSpec((WROWS, L), lambda i: (i, 0)),
        out_shape=jax.ShapeDtypeStruct((1024, L), jnp.bfloat16),
        compiler_params=pltpu.CompilerParams(vmem_limit_bytes=48 * MB),
        cost_estimate=cost(6.0),
        name="normalize",
    )(
        rows,
        valid,
        jnp.asarray(band_np(L, RAMW)),
        jnp.asarray(taper_np()[None, :]),
        jnp.asarray(inverse_count_np(L, RAMW)[None, :]),
    )


def whiten_kernel(x_ref, root_ref, dft_ref, bband_ref, bcount_ref, out0, out1, out23, held):
    step = pl.program_id(0)
    spectrum = dot(dft_ref[...], x_ref[...], ((1,), (1,)))
    real, imag = spectrum[:BINS], spectrum[BINS:]
    power = real * real + imag * imag
    high = power.astype(jnp.bfloat16)
    low = (power - high.astype(jnp.float32)).astype(jnp.bfloat16)
    smooth = (dot(bband_ref[...], high) + dot(bband_ref[...], low)) * bcount_ref[...]
    factor = lax.rsqrt(smooth + 1e-06) * root_ref[...]
    real, imag = real * factor, imag * factor
    first = lanes((BINS, 128)) < 64
    for tile in range(WROWS // 128):
        re = real[:, tile * 128 : (tile + 1) * 128]
        im = imag[:, tile * 128 : (tile + 1) * 128]
        at = step * (WROWS // 64) + tile * 2
        held[pl.ds(at, 1)] = jnp.where(first, re, pltpu.roll(im, 64, 1))[None]
        held[pl.ds(at + 1, 1)] = jnp.where(first, pltpu.roll(re, 64, 1), im)[None]

    @pl.when(step == pl.num_programs(0) - 1)
    def _():
        for block in range(BINS // 64):
            part = held[:, block * 64 : (block + 1) * 64, :]
            part = jnp.swapaxes(part, 0, 1).astype(jnp.bfloat16).reshape(2, 32, 16, 128)
            out0[block * 2 : block * 2 + 2] = part[:, :NF]
            out1[block * 2 : block * 2 + 2] = part[:, NF : 2 * NF]
            out23[block * 2 : block * 2 + 2] = part[:, 2 * NF :]


def whiten(rows, root):
    return pl.pallas_call(
        whiten_kernel,
        grid=(1024 // WROWS,),
        in_specs=[
            pl.BlockSpec((WROWS, L), lambda i: (i, 0)),
            pl.BlockSpec((1, WROWS), lambda i: (0, i)),
            whole(2 * BINS, L),
            whole(BINS, BINS),
            whole(BINS, 1),
        ],
        out_specs=[whole(16, NF, 16, 128), whole(16, NF, 16, 128), whole(16, 2 * NF, 16, 128)],
        out_shape=[
            jax.ShapeDtypeStruct((16, NF, 16, 128), jnp.bfloat16),
            jax.ShapeDtypeStruct((16, NF, 16, 128), jnp.bfloat16),
            jax.ShapeDtypeStruct((16, 2 * NF, 16, 128), jnp.bfloat16),
        ],
        scratch_shapes=[pltpu.VMEM((16, BINS, 128), jnp.float32)],
        compiler_params=pltpu.CompilerParams(vmem_limit_bytes=48 * MB),
        cost_estimate=cost(9.0),
        name="whiten",
    )(
        rows,
        root,
        jnp.asarray(dft_rows_np()),
        jnp.asarray(band_np(BINS, SMW)),
        jnp.asarray(inverse_count_np(BINS, SMW)[:, None]),
    )


def assemble_kernel(piece_ref, out_ref):
    count = piece_ref.shape[1]
    pieces = []
    for y in range(4):
        both = [piece_ref[h * 4 + y].astype(jnp.float32) for h in range(4)]
        pieces.append(jnp.stack(both, axis=1).reshape(count * 64, 128))
    group = lanes((count * 64, 128)) // 32
    for part in range(2):
        for bit in range(2):
            block = part * 2 + bit
            total = None
            for y in range(4):
                shift = (32 * (y - block)) % 128
                moved = pieces[y] if shift == 0 else pltpu.roll(pieces[y], shift, 1)
                total = moved if total is None else jnp.where(group == y, moved, total)
            out_ref[:, bit * 64 : (bit + 1) * 64, part * 128 : (part + 1) * 128] = total.reshape(
                count, 64, 128
            ).astype(jnp.bfloat16)


def assemble(pieces, part):
    return pl.pallas_call(
        assemble_kernel,
        grid=(1,),
        in_specs=[pl.BlockSpec((16, NF, 16, 128), lambda i: (0, part, 0, 0))],
        out_specs=whole(NF, 128, 256),
        out_shape=jax.ShapeDtypeStruct((NF, 128, 256), jnp.bfloat16),
        compiler_params=pltpu.CompilerParams(vmem_limit_bytes=32 * MB),
        cost_estimate=cost(0.8),
        name="assemble",
    )(pieces)


def own_side(own):
    return jnp.concatenate([own[:, :128].T, own[:, 128:].T], axis=1)


def visiting_side(block, spread):
    wide = dot(block, spread).astype(jnp.bfloat16)
    return jnp.concatenate([wide[:, :256], wide[:, 256:]], axis=0)


def cross_kernel(own_ref, v1_ref, v2_ref, v3_ref, v4_ref, spread_ref, out, held, zero_stop, wide):
    group = lanes((32, 256)) // 64
    first = lanes((32, 128)) < 64
    for d, visitor in enumerate((own_ref, v1_ref, v2_ref, v3_ref, v4_ref)):
        wide[d] = dot(visitor[...].reshape(NF * 128, 256), spread_ref[...]).astype(jnp.bfloat16)

    def right(d, f):
        rows = wide[d, f * 128 : (f + 1) * 128]
        return jnp.concatenate([rows[:, :256], rows[:, 256:]], axis=0)

    for f in range(NF):
        left = own_side(own_ref[f])
        near = dot(left, right(0, f))
        far = dot(left, right(4, f))
        for m in range(1, 4):
            held[f, :, m * 256 : (m + 1) * 256] = dot(left, right(m, f))
        for g in range(4):
            at = slice(g * 32, (g + 1) * 32)
            held[f, at, :256] = jnp.where(group <= g, far[at], near[at])
            tile = near[at, (g // 2) * 128 : (g // 2 + 1) * 128]
            turned = pltpu.roll(tile, 64, 1)
            zero_stop[f, at, :] = jnp.where(first, tile, turned) if g % 2 == 0 else jnp.where(first, turned, tile)
    pair = lanes((16, NF, 128)) < 64
    for g in range(4):
        for i in range(0, 32, 8):
            rows = jnp.swapaxes(held[:, g * 32 + i : g * 32 + i + 8, :], 0, 1)
            out[g, i * NF : (i + 8) * NF, :] = rows.reshape(8 * NF, 1024).astype(jnp.bfloat16)
        rows = jnp.swapaxes(zero_stop[:, g * 32 : (g + 1) * 32, :], 0, 1).reshape(16, 2, NF, 128)
        rows = jnp.where(pair, rows[:, 0], rows[:, 1])
        for u in range(8):
            both = jnp.concatenate([rows[2 * u], rows[2 * u + 1]], axis=0)
            out[g, 32 * NF :, u * 128 : (u + 1) * 128] = both.astype(jnp.bfloat16)


def cross(own, visitors):
    return pl.pallas_call(
        cross_kernel,
        grid=(1,),
        in_specs=[whole(NF, 128, 256) for _ in range(5)] + [whole(256, 512)],
        out_specs=whole(4, 34 * NF, 1024),
        scratch_shapes=[
            pltpu.VMEM((NF, 128, 1024), jnp.float32),
            pltpu.VMEM((NF, 128, 128), jnp.float32),
            pltpu.VMEM((5, NF * 128, 512), jnp.bfloat16),
        ],
        out_shape=jax.ShapeDtypeStruct((4, 34 * NF, 1024), jnp.bfloat16),
        compiler_params=pltpu.CompilerParams(vmem_limit_bytes=60 * MB),
        cost_estimate=cost(10.0),
        name="cross",
    )(own, *visitors, jnp.asarray(spread_np()))


def outer_kernel(own_ref, v4_ref, spread_ref, out, held, zero_stop, wide):
    group = lanes((32, 256)) // 64
    first = lanes((32, 128)) < 64
    for d, visitor in enumerate((own_ref, v4_ref)):
        wide[d] = dot(visitor[...].reshape(NF * 128, 256), spread_ref[...]).astype(jnp.bfloat16)

    def right(d, f):
        rows = wide[d, f * 128 : (f + 1) * 128]
        return jnp.concatenate([rows[:, :256], rows[:, 256:]], axis=0)

    for f in range(NF):
        left = own_side(own_ref[f])
        near = dot(left, right(0, f))
        far = dot(left, right(1, f))
        for g in range(4):
            at = slice(g * 32, (g + 1) * 32)
            held[f, at, :] = jnp.where(group <= g, far[at], near[at])
            tile = near[at, (g // 2) * 128 : (g // 2 + 1) * 128]
            turned = pltpu.roll(tile, 64, 1)
            zero_stop[f, at, :] = jnp.where(first, tile, turned) if g % 2 == 0 else jnp.where(first, turned, tile)
    pair = lanes((16, NF, 128)) < 64
    for g in range(4):
        for i in range(0, 32, 8):
            rows = jnp.swapaxes(held[:, g * 32 + i : g * 32 + i + 8, :], 0, 1)
            out[g, i * NF : (i + 8) * NF, :] = rows.reshape(8 * NF, 256).astype(jnp.bfloat16)
        rows = jnp.swapaxes(zero_stop[:, g * 32 : (g + 1) * 32, :], 0, 1).reshape(16, 2, NF, 128)
        rows = jnp.where(pair, rows[:, 0], rows[:, 1]).reshape(16 * NF, 128)
        out[g, 32 * NF :, :128] = rows[: 8 * NF].astype(jnp.bfloat16)
        out[g, 32 * NF :, 128:] = rows[8 * NF :].astype(jnp.bfloat16)


def inner_kernel(own_ref, v1_ref, v2_ref, v3_ref, spread_ref, out, held, wide):
    for d, visitor in enumerate((v1_ref, v2_ref, v3_ref)):
        wide[d] = dot(visitor[...].reshape(NF * 128, 256), spread_ref[...]).astype(jnp.bfloat16)
    for f in range(NF):
        left = own_side(own_ref[f])
        for m in range(3):
            rows = wide[m, f * 128 : (f + 1) * 128]
            right = jnp.concatenate([rows[:, :256], rows[:, 256:]], axis=0)
            held[f, :, m * 256 : (m + 1) * 256] = dot(left, right)
    for g in range(4):
        for i in range(0, 32, 8):
            rows = jnp.swapaxes(held[:, g * 32 + i : g * 32 + i + 8, :], 0, 1)
            out[g, i * NF : (i + 8) * NF, :] = rows.reshape(8 * NF, 768).astype(jnp.bfloat16)


def early(kernel, name, us, shape, scratch, *blocks):
    return pl.pallas_call(
        kernel,
        grid=(1,),
        in_specs=[whole(NF, 128, 256) for _ in blocks] + [whole(256, 512)],
        out_specs=whole(*shape),
        scratch_shapes=scratch,
        out_shape=jax.ShapeDtypeStruct(shape, jnp.bfloat16),
        compiler_params=pltpu.CompilerParams(vmem_limit_bytes=60 * MB),
        cost_estimate=cost(us),
        name=name,
    )(*blocks, jnp.asarray(spread_np()))


def outer(own, opposite):
    scratch = [
        pltpu.VMEM((NF, 128, 256), jnp.float32),
        pltpu.VMEM((NF, 128, 128), jnp.float32),
        pltpu.VMEM((2, NF * 128, 512), jnp.bfloat16),
    ]
    return early(outer_kernel, "outer", 3.0, (4, 40 * NF, 256), scratch, own, opposite)


def inner(own, visitors):
    scratch = [
        pltpu.VMEM((NF, 128, 768), jnp.float32),
        pltpu.VMEM((3, NF * 128, 512), jnp.bfloat16),
    ]
    return early(inner_kernel, "inner", 5.0, (4, 32 * NF, 768), scratch, own, *visitors)


STEP = 4


def finish_kernel(y_ref, mask_ref, mask0_ref, outer_ref, outer0_ref, inner_ref, *rest):
    pieces, zeros, (out_ref, held, held0) = rest[: PARTS - 1], rest[PARTS - 1 : 2 * PARTS - 2], rest[2 * PARTS - 2 :]
    step = pl.program_id(0)
    y = y_ref[0]
    lane_at = pl.multiple_of(step * 128, 128)
    first_at = pl.multiple_of(step // 4 * 128, 128)
    for source in range(4):
        row = slice(source * 32, source * 32 + NF)
        both = outer_ref[source].astype(jnp.float32)
        others = inner_ref[source].astype(jnp.float32)
        for i in range(STEP):
            held[i, row, :256] = both[i * NF : (i + 1) * NF]
            held[i, row, 256:] = others[i * NF : (i + 1) * NF]
        both = outer0_ref[source, :, pl.ds(first_at, 128)].astype(jnp.float32)
        for pair in range(2):
            held0[pair, row, :] = both[pair * NF : (pair + 1) * NF]
        for part in range(1, PARTS):
            row = slice(source * 32 + part * NF, source * 32 + (part + 1) * NF)
            both = pieces[part - 1][source].astype(jnp.float32)
            for i in range(STEP):
                held[i, row, :] = both[i * NF : (i + 1) * NF]
            both = zeros[part - 1][source, :, pl.ds(lane_at, 128)].astype(jnp.float32)
            for pair in range(2):
                held0[pair, row, :] = both[pair * NF : (pair + 1) * NF]
    for i in range(STEP):
        if i % 2 == 0:
            zero = (held0[i // 2] * mask0_ref[i // 2]).T.astype(jnp.bfloat16)
        out_ref[i * 1088 : i * 1088 + 64, :] = zero[i % 2 * 64 : (i % 2 + 1) * 64]
        for tile in range(8):
            at = slice(tile * 128, (tile + 1) * 128)
            block = (held[i, :, at] * mask_ref[0, i : i + 1, at]).T.astype(jnp.bfloat16)
            for half in range(2):
                stop = lax.rem(tile * 2 + half + 15 - y, 16) + 1
                out_ref[pl.ds(pl.multiple_of(i * 1088 + stop * 64, 64), 64), :] = block[half * 64 : (half + 1) * 64]


def finish(y, mask, mask0, outer, inner, pieces):
    return pl.pallas_call(
        finish_kernel,
        grid_spec=pltpu.PrefetchScalarGridSpec(
            num_scalar_prefetch=1,
            grid=(32 // STEP,),
            in_specs=[
                pl.BlockSpec((1, STEP, 1024), lambda i, y: (i, 0, 0)),
                pl.BlockSpec((STEP // 2, 1, 128), lambda i, y: (i, 0, 0)),
            ]
            + [
                pl.BlockSpec((4, STEP * NF, 256), lambda i, y: (0, i, 0)),
                pl.BlockSpec((4, 2 * NF, 256), lambda i, y: (0, 16 + i % 4, 0)),
                pl.BlockSpec((4, STEP * NF, 768), lambda i, y: (0, i, 0)),
            ]
            + [pl.BlockSpec((4, STEP * NF, 1024), lambda i, y: (0, i, 0)) for _ in pieces]
            + [pl.BlockSpec((4, 2 * NF, 1024), lambda i, y: (0, 16, 0)) for _ in pieces],
            out_specs=pl.BlockSpec((STEP * 1088, 128), lambda i, y: (i, 0)),
            scratch_shapes=[
                pltpu.VMEM((STEP, 128, 1024), jnp.float32),
                pltpu.VMEM((STEP // 2, 128, 128), jnp.float32),
            ],
        ),
        out_shape=jax.ShapeDtypeStruct((34816, 128), jnp.bfloat16),
        compiler_params=pltpu.CompilerParams(vmem_limit_bytes=60 * MB),
        cost_estimate=cost(9.0),
        name="finish",
    )(y, mask, mask0, outer, outer, inner, *pieces, *pieces)


def shift(block, axis, distance):
    size = lax.axis_size(axis)
    return lax.ppermute(block, axis, [(i, (i + distance) % size) for i in range(size)])


def tie(block, after):
    return block if after is None else lax.optimization_barrier((block, after))[0]


def hour_sum(value):
    total = value
    for zh, core in ((0, 1), (1, 0), (1, 1)):
        route = [(i, i ^ (zh * 2 + core)) for i in range(4)]
        total = total + lax.ppermute(value, ("zh", "core"), route)
    return total


def body(samples, gap_starts, valid_counts, owners, pair_mask):
    places = jnp.arange(L, dtype=jnp.int32)
    inside = places[None, :] < valid_counts[:, None]
    starts = gap_starts[:, :, None]
    holes = jnp.any((places[None, None, :] >= starts) & (places[None, None, :] < starts + GAPW), axis=1)
    valid = (inside & jnp.logical_not(holes)).astype(jnp.float32)
    member = (owners == jnp.arange(HGROUPS, dtype=jnp.int32)[None, :]).astype(jnp.float32)
    group_size = hour_sum(jnp.sum(member, axis=0))
    weight = jnp.sum(member / (HGROUPS * group_size)[None, :], axis=1)
    root = jnp.repeat(jnp.sqrt(weight), 32)[None, :]

    y = lax.axis_index("y").astype(jnp.int32)
    y_arg = y[None]
    mask = jnp.repeat(pair_mask.astype(jnp.float32), 2, axis=2)
    mask0 = mask[:, 0].reshape(16, 1, 128)
    mask = jnp.roll(mask[:, 1:], y + 1, axis=1).reshape(32 // STEP, STEP, 1024)

    spectra = whiten(normalize(samples.reshape(1024, L), valid), root)

    def transpose(block, after, name):
        with jax.named_scope(name):
            return lax.all_to_all(tie(block, after), ("zh", "core", "y"), 0, 0, tiled=True)

    def swap(part):
        with jax.named_scope(f"z{part}"):
            return shift(owns[part], "zl", 1)

    p0 = transpose(spectra[0], None, "p0")
    p1 = transpose(spectra[1], p0, "p1")
    x = lax.axis_index("x")

    def exchange(block, name):
        with jax.named_scope(name):
            return lax.all_to_all(block, "y", 0, 0, tiled=True)

    def choose(part):
        with jax.named_scope(f"x{part}"):
            return lax.optimization_barrier([jnp.where(x < d, swapped[part], owns[part]) for d in (1, 2, 3)])

    def gather(part, blocks, before, last):
        with jax.named_scope(f"x{part}"):
            return [shift(tie(block, last if d == 2 else before), "x", -d) for d, block in zip((1, 2, 3), blocks)]

    def do_cross(part, visitors, after):
        return cross(tie(owns[part], after), (*visitors, swapped[part]))

    owns = [assemble(p0, 0)]
    swapped = [swap(0)]
    chosen = choose(0)
    v0 = gather(0, chosen, None, None)
    a0 = outer(tie(owns[0], chosen), swapped[0])
    ya0 = exchange(tie(a0, p1), "yA0")
    owns.append(assemble(tie(p1, chosen), 0))
    swapped.append(swap(1))
    p23 = transpose(spectra[2], ya0, "p23")
    owns += [assemble(p23, 0), assemble(p23, 1)]
    swapped += [swap(2), swap(3)]
    c0 = inner(owns[0], v0)
    y0 = exchange(tie(c0, p23), "y0")
    v1 = gather(1, choose(1), None, c0)
    c1 = do_cross(1, v1, (c0, owns[2], owns[3]))
    y1 = exchange(tie(c1, y0), "y1")
    v2 = gather(2, choose(2), v0, c1)
    c2 = do_cross(2, v2, (c1, y0))
    y2 = exchange(tie(c2, y1), "y2")
    v3 = gather(3, choose(3), v1, c2)
    c3 = do_cross(3, v3, (c2, y1))
    y3 = exchange(tie(c3, y2), "y3")
    return finish(y_arg, mask, mask0, ya0, y0, (y1, y2, y3)).reshape(32, 17, 32, 2, 128)


def solution(mesh):
    fine = Mesh(mesh.devices.reshape(2, 4, 4, 2, 2), ("zl", "x", "y", "zh", "core"))
    chan, hour = ("zl", "x", "y"), ("zh", "core")
    placed = (
        P(hour, chan, None),
        P(hour, None),
        P(hour),
        P(hour, None),
        P(chan, None, None),
    )
    return jax.shard_map(
        body,
        mesh=fine,
        in_specs=placed,
        out_specs=P(chan, None, None, None, hour),
        check_vma=False,
    )
```

profile of v0, /device:TPU:1, one launch (start us, length us, event | category | flops | bytes accessed | tf_op | source)
XLA Modules:
  0.0 239.9 jit_solution(18323292692442439698)
XLA Ops:
  1.3 5.0 %collective-permute-start.2 = (f32[8]{0:T(128)}, f32[8]{0:T(128)}, u32[]{:S(2)}, u32[]{:S(2)}) collective-permute-start(f32[8]{0:T(128)} %convert_reduce_fusion), channel_id=1, source_target_pairs={{0,3},{1,2},{2,1},{3,0},{4,7},{5,6},{6,5},{7,4},{8,11},{9,10},{10,... | collective-permute-start | bytes 104 | tf_op jit(solution)/shard_map/ppermute | solution.py:418
  12.0 4.4 %normalize.1.x_ref = bf16[1024,1024]{1,0:T(8,128)(2,1)S(1)} custom-call(bf16[1024,1024]{1,0:T(8,128)(2,1)S(1)} %bitcast.7, f32[32,1024]{1,0:T(8,128)S(1)} %fusion.4.valid_ref, bf16[1024,1024]{1,0:T(8,128)(2,1)} %constant.59.clone.band_ref, f32[1,1024]{1,0:T(1,128)S(1)} %copy-done.5, f32[1,1024]{1,0:T(1,128)S(1)} %copy-done.4), custom_call_target="tpu_custom_call" | custom-call | flops 206999994368 | bytes 648000000 | tf_op jit(solution)/shard_map/normalize/pallas_call | solution.py:83
  17.4 8.7 %whiten.1 = (bf16[16,8,16,128]{3,2,1,0:T(8,128)(2,1)S(1)}, bf16[16,8,16,128]{3,2,1,0:T(8,128)(2,1)}, bf16[16,16,16,128]{3,2,1,0:T(8,128)(2,1)}) custom-call(bf16[1024,1024]{1,0:T(8,128)(2,1)S(1)} %normalize.1.x_ref, f32[1,1024]{1,0:T(1,128)S(1)} %broadcast_in_dim_reshape.3.root_ref, bf16[1024,1024]{1,0:T(8,128)(2,1)} %constant.62.clone.dft_ref, ...), custom_call_target="tpu_custom_call" | custom-call | flops 310499999744 | bytes 972000000 | tf_op jit(solution)/shard_map/whiten/pallas_call | solution.py:136
  26.1 17.7 %all_to_all.40.piece_ref = bf16[16,8,16,128]{3,2,1,0:T(8,128)(2,1)S(1)} all-to-all(bf16[16,8,16,128]{3,2,1,0:T(8,128)(2,1)S(1)} %get-tuple-element.39), channel_id=1, replica_groups=mesh['zl'=2,'x'=4,'y'=4,'zh'=2,'core'=2] {'zh','core','y'}, dimensions={0} | all-to-all | bytes 1048576 | tf_op jit(solution)/shard_map/p0/all_to_all | solution.py:443
  45.1 5.5 %all-to-all-start.1 = ((bf16[16,8,16,128]{3,2,1,0:T(8,128)(2,1)}), bf16[16,8,16,128]{3,2,1,0:T(8,128)(2,1)S(1)}, u32[]{:S(2)}, u32[]{:S(2)}) async-start(bf16[16,8,16,128]{3,2,1,0:T(8,128)(2,1)} %get-tuple-element.45), calls=%async_computation.1 | async-start | bytes 1048576 | tf_op jit(solution)/shard_map/p1/all_to_all | solution.py:443
  50.6 9.8 %collective-permute-done.3.v4_ref = bf16[8,128,256]{2,1,0:T(8,128)(2,1)S(1)} collective-permute-done((bf16[8,128,256]{2,1,0:T(8,128)(2,1)S(1)}, bf16[8,128,256]{2,1,0:T(8,128)(2,1)S(1)}, u32[]{:S(2)}, u32[]{:S(2)}) %collective-permute-start.3) | collective-permute-done | bytes 524320 | tf_op jit(solution)/shard_map/z0/ppermute | solution.py:407
  60.5 2.5 %collective-permute-start.4 = (bf16[8,128,256]{2,1,0:T(8,128)(2,1)S(1)}, bf16[8,128,256]{2,1,0:T(8,128)(2,1)}, u32[]{:S(2)}, u32[]{:S(2)}) collective-permute-start(bf16[8,128,256]{2,1,0:T(8,128)(2,1)S(1)} %get-tuple-element.40), channel_id=1, source_target_pairs={{0,48},{16,0},{32,16},{48,32},{1,49},{17,1},{33,17},{49,33},{2,50}... | collective-permute-start | bytes 1572872 | tf_op jit(solution)/shard_map/x0/ppermute | solution.py:407
  65.3 3.4 %outer.1 = bf16[4,320,256]{2,1,0:T(8,128)(2,1)} custom-call(bf16[8,128,256]{2,1,0:T(8,128)(2,1)} %copy-done, bf16[8,128,256]{2,1,0:T(8,128)(2,1)} %copy-done.9, bf16[256,512]{1,0:T(8,128)(2,1)} %constant.65.clone.spread_ref), custom_call_target="tpu_custom_call" | custom-call | flops 103499997184 | bytes 324000000 | tf_op jit(solution)/shard_map/outer/pallas_call | solution.py:306
  68.6 3.7 %all-to-all-start.2 = ((bf16[4,320,256]{2,1,0:T(8,128)(2,1)}), bf16[4,320,256]{2,1,0:T(8,128)(2,1)S(1)}, u32[]{:S(2)}, u32[]{:S(2)}) async-start(bf16[4,320,256]{2,1,0:T(8,128)(2,1)} %outer.1), calls=%async_computation.2 | async-start | bytes 1310720 | tf_op jit(solution)/shard_map/yA0/all_to_all | solution.py:455
  74.4 6.2 %all-to-all-done.2.outer_ref.outer0_ref = bf16[4,320,256]{2,1,0:T(8,128)(2,1)S(1)} async-done(((bf16[4,320,256]{2,1,0:T(8,128)(2,1)}), bf16[4,320,256]{2,1,0:T(8,128)(2,1)S(1)}, u32[]{:S(2)}, u32[]{:S(2)}) %all-to-all-start.2) | async-done | bytes 655392 | tf_op jit(solution)/shard_map/yA0/all_to_all | solution.py:455
  80.6 7.7 %all-to-all-start.3 = ((bf16[16,16,16,128]{3,2,1,0:T(8,128)(2,1)}), bf16[16,16,16,128]{3,2,1,0:T(8,128)(2,1)}, u32[]{:S(2)}, u32[]{:S(2)}) async-start(bf16[16,16,16,128]{3,2,1,0:T(8,128)(2,1)} %get-tuple-element.48), calls=%async_computation.3 | async-start | bytes 2097152 | tf_op jit(solution)/shard_map/p23/all_to_all | solution.py:443
  89.7 4.8 %inner.1 = bf16[4,256,768]{2,1,0:T(8,128)(2,1)} custom-call(bf16[8,128,256]{2,1,0:T(8,128)(2,1)} %copy-done, bf16[8,128,256]{2,1,0:T(8,128)(2,1)} %collective-permute-done.4.v1_ref, bf16[8,128,256]{2,1,0:T(8,128)(2,1)} %collective-permute-done.5.v2_ref, bf16[8,128,256]{2,1,0:T(8,128)(2,1)} %collective-permute-done.6.v3_ref, ...), custom_call_target="tpu_custom_call" | custom-call | flops 172499992576 | bytes 540000000 | tf_op jit(solution)/shard_map/inner/pallas_call | solution.py:306
  98.4 5.5 %all-to-all-done.3.piece_ref = bf16[16,16,16,128]{3,2,1,0:T(8,128)(2,1)} async-done(((bf16[16,16,16,128]{3,2,1,0:T(8,128)(2,1)}), bf16[16,16,16,128]{3,2,1,0:T(8,128)(2,1)}, u32[]{:S(2)}, u32[]{:S(2)}) %all-to-all-start.3) | async-done | bytes 1048608 | tf_op jit(solution)/shard_map/p23/all_to_all | solution.py:443
  103.9 2.4 assemble.6.own_ref
  107.0 2.4 assemble.7.own_ref
  110.1 4.4 %all-to-all-start.4 = ((bf16[4,256,768]{2,1,0:T(8,128)(2,1)}), bf16[4,256,768]{2,1,0:T(8,128)(2,1)}, u32[]{:S(2)}, u32[]{:S(2)}) async-start(bf16[4,256,768]{2,1,0:T(8,128)(2,1)} %inner.1), calls=%async_computation.4 | async-start | bytes 3145728 | tf_op jit(solution)/shard_map/y0/all_to_all | solution.py:455
  114.5 5.7 %collective-permute-done.8.v1_ref = bf16[8,128,256]{2,1,0:T(8,128)(2,1)S(1)} collective-permute-done((bf16[8,128,256]{2,1,0:T(8,128)(2,1)S(1)}, bf16[8,128,256]{2,1,0:T(8,128)(2,1)S(1)}, u32[]{:S(2)}, u32[]{:S(2)}) %collective-permute-start.8) | collective-permute-done | bytes 524320 | tf_op jit(solution)/shard_map/x1/ppermute | solution.py:407
  120.2 2.4 collective-permute-done.10.v3_ref
  123.5 6.3 %cross.3 = bf16[4,272,1024]{2,1,0:T(8,128)(2,1)} custom-call(bf16[8,128,256]{2,1,0:T(8,128)(2,1)} %assemble.5.own_ref, bf16[8,128,256]{2,1,0:T(8,128)(2,1)} %copy-done.15, bf16[8,128,256]{2,1,0:T(8,128)(2,1)} %copy-done.14, bf16[8,128,256]{2,1,0:T(8,128)(2,1)} %copy-done.16, bf16[8,128,256]{2,1,0:T(8,128)(2,1)} %collective-permute-done.7.v4_ref, ...), custom_call_target="tpu_custom_call" | custom-call | flops 344999985152 | bytes 1080000000 | tf_op jit(solution)/shard_map/cross/pallas_call | solution.py:242
  133.8 2.5 %broadcast_select_fusion = (bf16[8,128,256]{2,1,0:T(8,128)(2,1)}, bf16[8,128,256]{2,1,0:T(8,128)(2,1)}, bf16[8,128,256]{2,1,0:T(8,128)(2,1)}) fusion(bf16[8,128,256]{2,1,0:T(8,128)(2,1)} %collective-permute-done.15.v4_ref, bf16[8,128,256]{2,1,0:T(8,128)(2,1)} %assemble.7.own_ref, pred[]{:T(512)S(6)} %lt.63, pred[]{:T(512)S(6)} %lt.62, pred[]{:T(512)S(6)} %lt.61), kind=kLoop, calls=%fused_computation.7 | loop fusion | flops 786432 | bytes 2621443 | tf_op jit(solution)/shard_map/x3/jit(_where)/select_n | solution.py:459
  137.9 4.7 %all-to-all-start.5 = ((bf16[4,272,1024]{2,1,0:T(8,128)(2,1)}), bf16[4,272,1024]{2,1,0:T(8,128)(2,1)}, u32[]{:S(2)}, u32[]{:S(2)}) async-start(bf16[4,272,1024]{2,1,0:T(8,128)(2,1)} %cross.3), calls=%async_computation.5 | async-start | bytes 4456448 | tf_op jit(solution)/shard_map/y1/all_to_all | solution.py:455
  142.6 3.0 %collective-permute-done.14.v3_ref = bf16[8,128,256]{2,1,0:T(8,128)(2,1)S(1)} collective-permute-done((bf16[8,128,256]{2,1,0:T(8,128)(2,1)S(1)}, bf16[8,128,256]{2,1,0:T(8,128)(2,1)S(1)}, u32[]{:S(2)}, u32[]{:S(2)}) %collective-permute-start.14) | collective-permute-done | bytes 524320 | tf_op jit(solution)/shard_map/x2/ppermute | solution.py:407
  145.6 11.0 %collective-permute-done.13.v2_ref = bf16[8,128,256]{2,1,0:T(8,128)(2,1)S(1)} collective-permute-done((bf16[8,128,256]{2,1,0:T(8,128)(2,1)S(1)}, bf16[8,128,256]{2,1,0:T(8,128)(2,1)S(1)}, u32[]{:S(2)}, u32[]{:S(2)}) %collective-permute-start.13) | collective-permute-done | bytes 524320 | tf_op jit(solution)/shard_map/x2/ppermute | solution.py:407
  157.4 6.5 %cross.4 = bf16[4,272,1024]{2,1,0:T(8,128)(2,1)} custom-call(bf16[8,128,256]{2,1,0:T(8,128)(2,1)} %assemble.6.own_ref, bf16[8,128,256]{2,1,0:T(8,128)(2,1)} %copy-done.12, bf16[8,128,256]{2,1,0:T(8,128)(2,1)} %copy-done.13, bf16[8,128,256]{2,1,0:T(8,128)(2,1)} %copy-done.11, bf16[8,128,256]{2,1,0:T(8,128)(2,1)} %collective-permute-done.11.v4_ref, ...), custom_call_target="tpu_custom_call" | custom-call | flops 344999985152 | bytes 1080000000 | tf_op jit(solution)/shard_map/cross/pallas_call | solution.py:242
  164.6 4.9 %all-to-all-done.5.rest_0_.rest_3_ = bf16[4,272,1024]{2,1,0:T(8,128)(2,1)} async-done(((bf16[4,272,1024]{2,1,0:T(8,128)(2,1)}), bf16[4,272,1024]{2,1,0:T(8,128)(2,1)}, u32[]{:S(2)}, u32[]{:S(2)}) %all-to-all-start.5) | async-done | bytes 2228256 | tf_op jit(solution)/shard_map/y1/all_to_all | solution.py:455
  169.5 4.5 %all-to-all-start.6 = ((bf16[4,272,1024]{2,1,0:T(8,128)(2,1)}), bf16[4,272,1024]{2,1,0:T(8,128)(2,1)}, u32[]{:S(2)}, u32[]{:S(2)}) async-start(bf16[4,272,1024]{2,1,0:T(8,128)(2,1)} %cross.4), calls=%async_computation.6 | async-start | bytes 4456448 | tf_op jit(solution)/shard_map/y2/all_to_all | solution.py:455
  174.1 3.1 %collective-permute-done.17.v2_ref = bf16[8,128,256]{2,1,0:T(8,128)(2,1)S(1)} collective-permute-done((bf16[8,128,256]{2,1,0:T(8,128)(2,1)S(1)}, bf16[8,128,256]{2,1,0:T(8,128)(2,1)S(1)}, u32[]{:S(2)}, u32[]{:S(2)}) %collective-permute-start.17) | collective-permute-done | bytes 524320 | tf_op jit(solution)/shard_map/x3/ppermute | solution.py:407
  178.0 6.3 %cross.5 = bf16[4,272,1024]{2,1,0:T(8,128)(2,1)} custom-call(bf16[8,128,256]{2,1,0:T(8,128)(2,1)} %assemble.7.own_ref, bf16[8,128,256]{2,1,0:T(8,128)(2,1)} %collective-permute-done.16.v1_ref, bf16[8,128,256]{2,1,0:T(8,128)(2,1)} %copy-done.17, bf16[8,128,256]{2,1,0:T(8,128)(2,1)} %collective-permute-done.18.v3_ref, ...), custom_call_target="tpu_custom_call" | custom-call | flops 344999985152 | bytes 1080000000 | tf_op jit(solution)/shard_map/cross/pallas_call | solution.py:242
  184.3 15.3 %all-to-all-done.6.rest_1_.rest_4_ = bf16[4,272,1024]{2,1,0:T(8,128)(2,1)} async-done(((bf16[4,272,1024]{2,1,0:T(8,128)(2,1)}), bf16[4,272,1024]{2,1,0:T(8,128)(2,1)}, u32[]{:S(2)}, u32[]{:S(2)}) %all-to-all-start.6) | async-done | bytes 2228256 | tf_op jit(solution)/shard_map/y2/all_to_all | solution.py:455
  199.6 3.6 %all-to-all-start.7 = ((bf16[4,272,1024]{2,1,0:T(8,128)(2,1)}), bf16[4,272,1024]{2,1,0:T(8,128)(2,1)S(1)}, u32[]{:S(2)}, u32[]{:S(2)}) async-start(bf16[4,272,1024]{2,1,0:T(8,128)(2,1)} %cross.5), calls=%async_computation.7 | async-start | bytes 4456448 | tf_op jit(solution)/shard_map/y3/all_to_all | solution.py:455
  205.7 22.1 %all-to-all-done.7.rest_2_.rest_5_ = bf16[4,272,1024]{2,1,0:T(8,128)(2,1)S(1)} async-done(((bf16[4,272,1024]{2,1,0:T(8,128)(2,1)}), bf16[4,272,1024]{2,1,0:T(8,128)(2,1)S(1)}, u32[]{:S(2)}, u32[]{:S(2)}) %all-to-all-start.7) | async-done | bytes 2228256 | tf_op jit(solution)/shard_map/y3/all_to_all | solution.py:455
  229.2 10.8 %finish.1 = bf16[34816,128]{1,0:T(8,128)(2,1)} custom-call(s32[1]{0:T(128)} %bitcast.y_ref, f32[8,4,1024]{2,1,0:T(4,128)} %reshape.18.mask_ref, f32[16,1,128]{2,1,0:T(1,128)} %reshape_squeeze.3.mask0_ref, bf16[4,320,256]{2,1,0:T(8,128)(2,1)} %copy-done.7, bf16[4,320,256]{2,1,0:T(8,128)(2,1)} %copy-done.7, bf16[4,256,768]{2,1,0:T(8,128)(2,1)} %all-to-all-done.4.inner_ref, ...), custom_call_target="tpu_custom_call" | custom-call | flops 310499999744 | bytes 972000000 | tf_op jit(solution)/shard_map/finish/pallas_call | solution.py:376
  (94 shorter events, 33.0 us)
Async XLA Ops:
  1.3 15.1 %collective-permute-start.2 = (f32[8]{0:T(128)}, f32[8]{0:T(128)}, u32[]{:S(2)}, u32[]{:S(2)}) collective-permute-start(f32[8]{0:T(128)} %convert_reduce_fusion), channel_id=1, source_target_pairs={{0,3},{1,2},{2,1},{3,0},{4,7},{5,6},{6,5},{7,4},{8,11},{9,10},{10,... | collective-permute-start | bytes 104 | tf_op jit(solution)/shard_map/ppermute | solution.py:418
  6.3 10.1 %collective-permute-start.1 = (f32[8]{0:T(128)}, f32[8]{0:T(128)}, u32[]{:S(2)}, u32[]{:S(2)}) collective-permute-start(f32[8]{0:T(128)} %convert_reduce_fusion), channel_id=1, source_target_pairs={{0,2},{1,3},{2,0},{3,1},{4,6},{5,7},{6,4},{7,5},{8,10},{9,11},{10,... | collective-permute-start | bytes 104 | tf_op jit(solution)/shard_map/ppermute | solution.py:418
  6.3 10.1 %collective-permute-start = (f32[8]{0:T(128)}, f32[8]{0:T(128)}, u32[]{:S(2)}, u32[]{:S(2)}) collective-permute-start(f32[8]{0:T(128)} %convert_reduce_fusion), channel_id=1, source_target_pairs={{0,1},{1,0},{2,3},{3,2},{4,5},{5,4},{6,7},{7,6},{8,9},{9,8},{10,11... | collective-permute-start | bytes 104 | tf_op jit(solution)/shard_map/ppermute | solution.py:418
  44.3 20.9 %copy-start = (bf16[8,128,256]{2,1,0:T(8,128)(2,1)}, bf16[8,128,256]{2,1,0:T(8,128)(2,1)S(1)}, u32[]{:S(2)}) copy-start(bf16[8,128,256]{2,1,0:T(8,128)(2,1)S(1)} %assemble.4.own_ref) | copy-start | bytes 1572868
  44.3 16.1 %collective-permute-start.3 = (bf16[8,128,256]{2,1,0:T(8,128)(2,1)S(1)}, bf16[8,128,256]{2,1,0:T(8,128)(2,1)S(1)}, u32[]{:S(2)}, u32[]{:S(2)}) collective-permute-start(bf16[8,128,256]{2,1,0:T(8,128)(2,1)S(1)} %assemble.4.own_ref), channel_id=1, source_target_pairs={{0,64},{64,0},{1,65},{65,1},{2,66},{66,2},{3,67},{67,3},{4,68},{68... | collective-permute-start | bytes 1572872 | tf_op jit(solution)/shard_map/z0/ppermute | solution.py:407
  45.1 20.1 %all-to-all-start.1 = ((bf16[16,8,16,128]{3,2,1,0:T(8,128)(2,1)}), bf16[16,8,16,128]{3,2,1,0:T(8,128)(2,1)S(1)}, u32[]{:S(2)}, u32[]{:S(2)}) async-start(bf16[16,8,16,128]{3,2,1,0:T(8,128)(2,1)} %get-tuple-element.45), calls=%async_computation.1 | async-start | bytes 1048576 | tf_op jit(solution)/shard_map/p1/all_to_all | solution.py:443
  60.5 27.8 %collective-permute-start.4 = (bf16[8,128,256]{2,1,0:T(8,128)(2,1)S(1)}, bf16[8,128,256]{2,1,0:T(8,128)(2,1)}, u32[]{:S(2)}, u32[]{:S(2)}) collective-permute-start(bf16[8,128,256]{2,1,0:T(8,128)(2,1)S(1)} %get-tuple-element.40), channel_id=1, source_target_pairs={{0,48},{16,0},{32,16},{48,32},{1,49},{17,1},{33,17},{49,33},{2,50}... | collective-permute-start | bytes 1572872 | tf_op jit(solution)/shard_map/x0/ppermute | solution.py:407
  63.1 25.2 %collective-permute-start.5 = (bf16[8,128,256]{2,1,0:T(8,128)(2,1)S(1)}, bf16[8,128,256]{2,1,0:T(8,128)(2,1)}, u32[]{:S(2)}, u32[]{:S(2)}) collective-permute-start(bf16[8,128,256]{2,1,0:T(8,128)(2,1)S(1)} %get-tuple-element.41), channel_id=1, source_target_pairs={{0,32},{16,48},{32,0},{48,16},{1,33},{17,49},{33,1},{49,17},{2,34}... | collective-permute-start | bytes 1572872 | tf_op jit(solution)/shard_map/x0/ppermute | solution.py:407
  63.6 26.2 %collective-permute-start.6 = (bf16[8,128,256]{2,1,0:T(8,128)(2,1)S(1)}, bf16[8,128,256]{2,1,0:T(8,128)(2,1)}, u32[]{:S(2)}, u32[]{:S(2)}) collective-permute-start(bf16[8,128,256]{2,1,0:T(8,128)(2,1)S(1)} %get-tuple-element.42), channel_id=1, source_target_pairs={{0,16},{16,32},{32,48},{48,0},{1,17},{17,33},{33,49},{49,1},{2,18}... | collective-permute-start | bytes 1572872 | tf_op jit(solution)/shard_map/x0/ppermute | solution.py:407
  68.6 12.0 %all-to-all-start.2 = ((bf16[4,320,256]{2,1,0:T(8,128)(2,1)}), bf16[4,320,256]{2,1,0:T(8,128)(2,1)S(1)}, u32[]{:S(2)}, u32[]{:S(2)}) async-start(bf16[4,320,256]{2,1,0:T(8,128)(2,1)} %outer.1), calls=%async_computation.2 | async-start | bytes 1310720 | tf_op jit(solution)/shard_map/yA0/all_to_all | solution.py:455
  73.7 20.8 %collective-permute-start.7 = (bf16[8,128,256]{2,1,0:T(8,128)(2,1)}, bf16[8,128,256]{2,1,0:T(8,128)(2,1)}, u32[]{:S(2)}, u32[]{:S(2)}) collective-permute-start(bf16[8,128,256]{2,1,0:T(8,128)(2,1)} %assemble.5.own_ref), channel_id=1, source_target_pairs={{0,64},{64,0},{1,65},{65,1},{2,66},{66,2},{3,67},{67,3},{4,68},{68... | collective-permute-start | bytes 1572872 | tf_op jit(solution)/shard_map/z1/ppermute | solution.py:407
  80.6 13.9 %copy-start.7 = (bf16[4,320,256]{2,1,0:T(8,128)(2,1)}, bf16[4,320,256]{2,1,0:T(8,128)(2,1)S(1)}, u32[]{:S(2)}) copy-start(bf16[4,320,256]{2,1,0:T(8,128)(2,1)S(1)} %all-to-all-done.2.outer_ref.outer0_ref) | copy-start | bytes 1966084
  80.6 23.3 %all-to-all-start.3 = ((bf16[16,16,16,128]{3,2,1,0:T(8,128)(2,1)}), bf16[16,16,16,128]{3,2,1,0:T(8,128)(2,1)}, u32[]{:S(2)}, u32[]{:S(2)}) async-start(bf16[16,16,16,128]{3,2,1,0:T(8,128)(2,1)} %get-tuple-element.48), calls=%async_computation.3 | async-start | bytes 2097152 | tf_op jit(solution)/shard_map/p23/all_to_all | solution.py:443
  95.8 18.6 %collective-permute-start.9 = (bf16[8,128,256]{2,1,0:T(8,128)(2,1)S(1)}, bf16[8,128,256]{2,1,0:T(8,128)(2,1)S(1)}, u32[]{:S(2)}, u32[]{:S(2)}) collective-permute-start(bf16[8,128,256]{2,1,0:T(8,128)(2,1)S(1)} %get-tuple-element.54), channel_id=1, source_target_pairs={{0,32},{16,48},{32,0},{48,16},{1,33},{17,49},{33,1},{49,17},{2,34}... | collective-permute-start | bytes 1572872 | tf_op jit(solution)/shard_map/x1/ppermute | solution.py:407
  96.9 23.3 %collective-permute-start.8 = (bf16[8,128,256]{2,1,0:T(8,128)(2,1)S(1)}, bf16[8,128,256]{2,1,0:T(8,128)(2,1)S(1)}, u32[]{:S(2)}, u32[]{:S(2)}) collective-permute-start(bf16[8,128,256]{2,1,0:T(8,128)(2,1)S(1)} %get-tuple-element.52), channel_id=1, source_target_pairs={{0,48},{16,0},{32,16},{48,32},{1,49},{17,1},{33,17},{49,33},{2,50}... | collective-permute-start | bytes 1572872 | tf_op jit(solution)/shard_map/x1/ppermute | solution.py:407
  98.4 24.2 %collective-permute-start.10 = (bf16[8,128,256]{2,1,0:T(8,128)(2,1)S(1)}, bf16[8,128,256]{2,1,0:T(8,128)(2,1)S(1)}, u32[]{:S(2)}, u32[]{:S(2)}) collective-permute-start(bf16[8,128,256]{2,1,0:T(8,128)(2,1)S(1)} %get-tuple-element.55), channel_id=1, source_target_pairs={{0,16},{16,32},{32,48},{48,0},{1,17},{17,33},{33,49},{49,1},{2,18}... | collective-permute-start | bytes 1572872 | tf_op jit(solution)/shard_map/x1/ppermute | solution.py:407
  106.2 23.5 %collective-permute-start.11 = (bf16[8,128,256]{2,1,0:T(8,128)(2,1)}, bf16[8,128,256]{2,1,0:T(8,128)(2,1)}, u32[]{:S(2)}, u32[]{:S(2)}) collective-permute-start(bf16[8,128,256]{2,1,0:T(8,128)(2,1)} %assemble.6.own_ref), channel_id=1, source_target_pairs={{0,64},{64,0},{1,65},{65,1},{2,66},{66,2},{3,67},{67,3},{4,68},{68... | collective-permute-start | bytes 1572872 | tf_op jit(solution)/shard_map/z2/ppermute | solution.py:407
  109.4 24.4 %collective-permute-start.15 = (bf16[8,128,256]{2,1,0:T(8,128)(2,1)}, bf16[8,128,256]{2,1,0:T(8,128)(2,1)}, u32[]{:S(2)}, u32[]{:S(2)}) collective-permute-start(bf16[8,128,256]{2,1,0:T(8,128)(2,1)} %assemble.7.own_ref), channel_id=1, source_target_pairs={{0,64},{64,0},{1,65},{65,1},{2,66},{66,2},{3,67},{67,3},{4,68},{68... | collective-permute-start | bytes 1572872 | tf_op jit(solution)/shard_map/z3/ppermute | solution.py:407
  110.1 27.8 %all-to-all-start.4 = ((bf16[4,256,768]{2,1,0:T(8,128)(2,1)}), bf16[4,256,768]{2,1,0:T(8,128)(2,1)}, u32[]{:S(2)}, u32[]{:S(2)}) async-start(bf16[4,256,768]{2,1,0:T(8,128)(2,1)} %inner.1), calls=%async_computation.4 | async-start | bytes 3145728 | tf_op jit(solution)/shard_map/y0/all_to_all | solution.py:455
  114.5 8.1 %copy-start.14 = (bf16[8,128,256]{2,1,0:T(8,128)(2,1)}, bf16[8,128,256]{2,1,0:T(8,128)(2,1)S(1)}, u32[]{:S(2)}) copy-start(bf16[8,128,256]{2,1,0:T(8,128)(2,1)S(1)} %collective-permute-done.9.v2_ref) | copy-start | bytes 1572868
  131.1 14.5 %collective-permute-start.14 = (bf16[8,128,256]{2,1,0:T(8,128)(2,1)S(1)}, bf16[8,128,256]{2,1,0:T(8,128)(2,1)S(1)}, u32[]{:S(2)}, u32[]{:S(2)}) collective-permute-start(bf16[8,128,256]{2,1,0:T(8,128)(2,1)S(1)} %get-tuple-element.63), channel_id=1, source_target_pairs={{0,16},{16,32},{32,48},{48,0},{1,17},{17,33},{33,49},{49,1},{2,18}... | collective-permute-start | bytes 1572872 | tf_op jit(solution)/shard_map/x2/ppermute | solution.py:407
  131.5 14.0 %collective-permute-start.12 = (bf16[8,128,256]{2,1,0:T(8,128)(2,1)S(1)}, bf16[8,128,256]{2,1,0:T(8,128)(2,1)S(1)}, u32[]{:S(2)}, u32[]{:S(2)}) collective-permute-start(bf16[8,128,256]{2,1,0:T(8,128)(2,1)S(1)} %get-tuple-element.59), channel_id=1, source_target_pairs={{0,48},{16,0},{32,16},{48,32},{1,49},{17,1},{33,17},{49,33},{2,50}... | collective-permute-start | bytes 1572872 | tf_op jit(solution)/shard_map/x2/ppermute | solution.py:407
  133.8 22.8 %collective-permute-start.13 = (bf16[8,128,256]{2,1,0:T(8,128)(2,1)S(1)}, bf16[8,128,256]{2,1,0:T(8,128)(2,1)S(1)}, u32[]{:S(2)}, u32[]{:S(2)}) collective-permute-start(bf16[8,128,256]{2,1,0:T(8,128)(2,1)S(1)} %get-tuple-element.61), channel_id=1, source_target_pairs={{0,32},{16,48},{32,0},{48,16},{1,33},{17,49},{33,1},{49,17},{2,34}... | collective-permute-start | bytes 1572872 | tf_op jit(solution)/shard_map/x2/ppermute | solution.py:407
  136.3 37.8 %collective-permute-start.16 = (bf16[8,128,256]{2,1,0:T(8,128)(2,1)}, bf16[8,128,256]{2,1,0:T(8,128)(2,1)}, u32[]{:S(2)}, u32[]{:S(2)}) collective-permute-start(bf16[8,128,256]{2,1,0:T(8,128)(2,1)} %get-tuple-element.67), channel_id=1, source_target_pairs={{0,48},{16,0},{32,16},{48,32},{1,49},{17,1},{33,17},{49,33},{2,50}... | collective-permute-start | bytes 1572872 | tf_op jit(solution)/shard_map/x3/ppermute | solution.py:407
  137.9 36.2 %collective-permute-start.18 = (bf16[8,128,256]{2,1,0:T(8,128)(2,1)}, bf16[8,128,256]{2,1,0:T(8,128)(2,1)}, u32[]{:S(2)}, u32[]{:S(2)}) collective-permute-start(bf16[8,128,256]{2,1,0:T(8,128)(2,1)} %get-tuple-element.71), channel_id=1, source_target_pairs={{0,16},{16,32},{32,48},{48,0},{1,17},{17,33},{33,49},{49,1},{2,18}... | collective-permute-start | bytes 1572872 | tf_op jit(solution)/shard_map/x3/ppermute | solution.py:407
  137.9 31.6 %all-to-all-start.5 = ((bf16[4,272,1024]{2,1,0:T(8,128)(2,1)}), bf16[4,272,1024]{2,1,0:T(8,128)(2,1)}, u32[]{:S(2)}, u32[]{:S(2)}) async-start(bf16[4,272,1024]{2,1,0:T(8,128)(2,1)} %cross.3), calls=%async_computation.5 | async-start | bytes 4456448 | tf_op jit(solution)/shard_map/y1/all_to_all | solution.py:455
  145.6 11.0 %copy-start.11 = (bf16[8,128,256]{2,1,0:T(8,128)(2,1)}, bf16[8,128,256]{2,1,0:T(8,128)(2,1)S(1)}, u32[]{:S(2)}) copy-start(bf16[8,128,256]{2,1,0:T(8,128)(2,1)S(1)} %collective-permute-done.14.v3_ref) | copy-start | bytes 1572868
  145.6 11.0 %copy-start.12 = (bf16[8,128,256]{2,1,0:T(8,128)(2,1)}, bf16[8,128,256]{2,1,0:T(8,128)(2,1)S(1)}, u32[]{:S(2)}) copy-start(bf16[8,128,256]{2,1,0:T(8,128)(2,1)S(1)} %collective-permute-done.12.v1_ref) | copy-start | bytes 1572868
  163.9 13.3 %collective-permute-start.17 = (bf16[8,128,256]{2,1,0:T(8,128)(2,1)S(1)}, bf16[8,128,256]{2,1,0:T(8,128)(2,1)S(1)}, u32[]{:S(2)}, u32[]{:S(2)}) collective-permute-start(bf16[8,128,256]{2,1,0:T(8,128)(2,1)S(1)} %copy-done.8), channel_id=1, source_target_pairs={{0,32},{16,48},{32,0},{48,16},{1,33},{17,49},{33,1},{49,17},{2,34}... | collective-permute-start | bytes 1572872 | tf_op jit(solution)/shard_map/x3/ppermute | solution.py:407
  169.5 30.1 %all-to-all-start.6 = ((bf16[4,272,1024]{2,1,0:T(8,128)(2,1)}), bf16[4,272,1024]{2,1,0:T(8,128)(2,1)}, u32[]{:S(2)}, u32[]{:S(2)}) async-start(bf16[4,272,1024]{2,1,0:T(8,128)(2,1)} %cross.4), calls=%async_computation.6 | async-start | bytes 4456448 | tf_op jit(solution)/shard_map/y2/all_to_all | solution.py:455
  184.3 19.0 %copy-start.10 = (s32[32,17,32]{2,0,1:T(8,128)S(1)}, s32[32,17,32]{2,0,1:T(8,128)}, u32[]{:S(2)}) copy-start(s32[32,17,32]{2,0,1:T(8,128)} %param.20) | copy-start | bytes 208900
  199.6 28.2 %all-to-all-start.7 = ((bf16[4,272,1024]{2,1,0:T(8,128)(2,1)}), bf16[4,272,1024]{2,1,0:T(8,128)(2,1)S(1)}, u32[]{:S(2)}, u32[]{:S(2)}) async-start(bf16[4,272,1024]{2,1,0:T(8,128)(2,1)} %cross.5), calls=%async_computation.7 | async-start | bytes 4456448 | tf_op jit(solution)/shard_map/y3/all_to_all | solution.py:455
  (13 other events, 36.4 us)
where the time goes:
time: 244 us; the launch traced here: 240 us
  waiting for transfers between devices  91.7 us (38%)
  Pallas kernels  57.6 us (24%)
  starting transfers between devices  53.8 us (22%)
  blocking collectives  17.7 us (7%)
  other arithmetic  9.75 us (4%)
  local copies, waits for them, and re-layouts  9.18 us (4%)
    all_to_all x5, waiting for transfers between devices, exchange(): return lax.all_to_all(block, 'y', 0, 0, tiled=True)  48.6 us
    ppermute x16, waiting for transfers between devices, shift(): lax.ppermute(block, axis, [(i, (i + distance) % size) for i in range(size)])  36.5 us
    all_to_all x5, starting transfers between devices, exchange(): return lax.all_to_all(block, 'y', 0, 0, tiled=True)  20.9 us
    pallas_call x3, Pallas kernels, cross(): pl.pallas_call(cross_kernel, grid=(1,), in_specs=[whole(NF, 128, 256) for...  19 us
    all_to_all x1, blocking collectives, transpose(): lax.all_to_all(tie(block, after), ('zh', 'core', 'y'), 0, 0, tiled=True)  17.7 us
    ppermute x16, starting transfers between devices, shift(): lax.ppermute(block, axis, [(i, (i + distance) % size) for i in range(size)])  14.3 us
    all_to_all x2, starting transfers between devices, transpose(): lax.all_to_all(tie(block, after), ('zh', 'core', 'y'), 0, 0, tiled=True)  13.1 us
    pallas_call x1, Pallas kernels, finish(): pl.pallas_call(finish_kernel, grid_spec=pltpu.PrefetchScalarGridSpec(num_...  10.8 us
  transfers between devices with their start and end apart: 26, of which 13 were waited for; matrix products, arithmetic and copies ran while one was open for 4% of the time, Pallas kernels for 16%

commit v1 on v0

--- a/solution.py
+++ b/solution.py
@@ -68,8 +68,14 @@
 WROWS = 512
 
 
-def level_kernel(x_ref, valid_ref, band_ref, taper_ref, icount_ref, out_ref):
-    x = x_ref[...].astype(jnp.float32).reshape(WROWS // 32, 32, L) * valid_ref[...][:, None, :]
+def level_kernel(x_ref, starts_ref, counts_ref, band_ref, taper_ref, icount_ref, out_ref):
+    places = lanes((WROWS // 32, L))
+    valid = places < counts_ref[...]
+    for gap in range(starts_ref.shape[1]):
+        start = starts_ref[:, gap : gap + 1]
+        valid = valid & ((places < start) | (places >= start + GAPW))
+    valid = valid.astype(jnp.float32)
+    x = x_ref[...].astype(jnp.float32).reshape(WROWS // 32, 32, L) * valid[:, None, :]
     x = x.reshape(WROWS, L)
     level = dot(jnp.abs(x).astype(jnp.bfloat16), band_ref[...]) * icount_ref[...]
     out_ref[...] = (taper_ref[...] * x / (level + 1e-06)).astype(jnp.bfloat16)
@@ -79,13 +85,14 @@
     return pl.BlockSpec(shape, lambda *i: (0,) * len(shape))
 
 
-def normalize(rows, valid):
+def normalize(rows, starts, counts):
     return pl.pallas_call(
         level_kernel,
         grid=(1024 // WROWS,),
         in_specs=[
             pl.BlockSpec((WROWS, L), lambda i: (i, 0)),
-            pl.BlockSpec((WROWS // 32, L), lambda i: (i, 0)),
+            pl.BlockSpec((WROWS // 32, starts.shape[1]), lambda i: (i, 0)),
+            pl.BlockSpec((WROWS // 32, 1), lambda i: (i, 0)),
             whole(L, L),
             whole(1, L),
             whole(1, L),
@@ -97,7 +104,8 @@
         name="normalize",
     )(
         rows,
-        valid,
+        starts,
+        counts,
         jnp.asarray(band_np(L, RAMW)),
         jnp.asarray(taper_np()[None, :]),
         jnp.asarray(inverse_count_np(L, RAMW)[None, :]),
@@ -162,8 +170,13 @@
     )
 
 
-def assemble_kernel(piece_ref, out_ref):
-    count = piece_ref.shape[1]
+def assemble_kernel(piece_ref, *out_refs):
+    for part, out_ref in enumerate(out_refs):
+        assemble_part(piece_ref.at[:, part * NF : (part + 1) * NF], out_ref)
+
+
+def assemble_part(piece_ref, out_ref):
+    count = NF
     pieces = []
     for y in range(4):
         both = [piece_ref[h * 4 + y].astype(jnp.float32) for h in range(4)]
@@ -182,15 +195,16 @@
             ).astype(jnp.bfloat16)
 
 
-def assemble(pieces, part):
+def assemble(pieces):
+    parts = pieces.shape[1] // NF
     return pl.pallas_call(
         assemble_kernel,
         grid=(1,),
-        in_specs=[pl.BlockSpec((16, NF, 16, 128), lambda i: (0, part, 0, 0))],
-        out_specs=whole(NF, 128, 256),
-        out_shape=jax.ShapeDtypeStruct((NF, 128, 256), jnp.bfloat16),
+        in_specs=[whole(*pieces.shape)],
+        out_specs=[whole(NF, 128, 256)] * parts,
+        out_shape=[jax.ShapeDtypeStruct((NF, 128, 256), jnp.bfloat16)] * parts,
         compiler_params=pltpu.CompilerParams(vmem_limit_bytes=32 * MB),
-        cost_estimate=cost(0.8),
+        cost_estimate=cost(0.8 * parts),
         name="assemble",
     )(pieces)
 
@@ -337,7 +351,7 @@
 
 
 def finish_kernel(y_ref, mask_ref, mask0_ref, outer_ref, outer0_ref, inner_ref, *rest):
-    pieces, zeros, (out_ref, held, held0) = rest[: PARTS - 1], rest[PARTS - 1 : 2 * PARTS - 2], rest[2 * PARTS - 2 :]
+    pieces, zeros, last, last0, (out_ref, held, held0) = rest[:2], rest[2:4], rest[4:8], rest[8:12], rest[12:]
     step = pl.program_id(0)
     y = y_ref[0]
     lane_at = pl.multiple_of(step * 128, 128)
@@ -352,7 +366,7 @@
         both = outer0_ref[source, :, pl.ds(first_at, 128)].astype(jnp.float32)
         for pair in range(2):
             held0[pair, row, :] = both[pair * NF : (pair + 1) * NF]
-        for part in range(1, PARTS):
+        for part in range(1, PARTS - 1):
             row = slice(source * 32 + part * NF, source * 32 + (part + 1) * NF)
             both = pieces[part - 1][source].astype(jnp.float32)
             for i in range(STEP):
@@ -360,6 +374,14 @@
             both = zeros[part - 1][source, :, pl.ds(lane_at, 128)].astype(jnp.float32)
             for pair in range(2):
                 held0[pair, row, :] = both[pair * NF : (pair + 1) * NF]
+    for s in range(4):
+        row = pl.ds(pl.multiple_of(lax.rem(y + 4 - s, 4) * 32 + (PARTS - 1) * NF, NF), NF)
+        both = last[s][...].astype(jnp.float32)
+        for i in range(STEP):
+            held[i, row, :] = both[i * NF : (i + 1) * NF]
+        both = last0[s][:, pl.ds(lane_at, 128)].astype(jnp.float32)
+        for pair in range(2):
+            held0[pair, row, :] = both[pair * NF : (pair + 1) * NF]
     for i in range(STEP):
         if i % 2 == 0:
             zero = (held0[i // 2] * mask0_ref[i // 2]).T.astype(jnp.bfloat16)
@@ -372,7 +394,7 @@
                 out_ref[pl.ds(pl.multiple_of(i * 1088 + stop * 64, 64), 64), :] = block[half * 64 : (half + 1) * 64]
 
 
-def finish(y, mask, mask0, outer, inner, pieces):
+def finish(y, mask, mask0, outer, inner, pieces, last):
     return pl.pallas_call(
         finish_kernel,
         grid_spec=pltpu.PrefetchScalarGridSpec(
@@ -388,7 +410,9 @@
                 pl.BlockSpec((4, STEP * NF, 768), lambda i, y: (0, i, 0)),
             ]
             + [pl.BlockSpec((4, STEP * NF, 1024), lambda i, y: (0, i, 0)) for _ in pieces]
-            + [pl.BlockSpec((4, 2 * NF, 1024), lambda i, y: (0, 16, 0)) for _ in pieces],
+            + [pl.BlockSpec((4, 2 * NF, 1024), lambda i, y: (0, 16, 0)) for _ in pieces]
+            + [pl.BlockSpec((STEP * NF, 1024), lambda i, y: (i, 0)) for _ in last]
+            + [pl.BlockSpec((2 * NF, 1024), lambda i, y: (16, 0)) for _ in last],
             out_specs=pl.BlockSpec((STEP * 1088, 128), lambda i, y: (i, 0)),
             scratch_shapes=[
                 pltpu.VMEM((STEP, 128, 1024), jnp.float32),
@@ -399,7 +423,7 @@
         compiler_params=pltpu.CompilerParams(vmem_limit_bytes=60 * MB),
         cost_estimate=cost(9.0),
         name="finish",
-    )(y, mask, mask0, outer, outer, inner, *pieces, *pieces)
+    )(y, mask, mask0, outer, outer, inner, *pieces, *pieces, *last, *last)
 
 
 def shift(block, axis, distance):
@@ -420,11 +444,6 @@
 
 
 def body(samples, gap_starts, valid_counts, owners, pair_mask):
-    places = jnp.arange(L, dtype=jnp.int32)
-    inside = places[None, :] < valid_counts[:, None]
-    starts = gap_starts[:, :, None]
-    holes = jnp.any((places[None, None, :] >= starts) & (places[None, None, :] < starts + GAPW), axis=1)
-    valid = (inside & jnp.logical_not(holes)).astype(jnp.float32)
     member = (owners == jnp.arange(HGROUPS, dtype=jnp.int32)[None, :]).astype(jnp.float32)
     group_size = hour_sum(jnp.sum(member, axis=0))
     weight = jnp.sum(member / (HGROUPS * group_size)[None, :], axis=1)
@@ -436,7 +455,7 @@
     mask0 = mask[:, 0].reshape(16, 1, 128)
     mask = jnp.roll(mask[:, 1:], y + 1, axis=1).reshape(32 // STEP, STEP, 1024)
 
-    spectra = whiten(normalize(samples.reshape(1024, L), valid), root)
+    spectra = whiten(normalize(samples.reshape(1024, L), gap_starts, valid_counts[:, None]), root)
 
     def transpose(block, after, name):
         with jax.named_scope(name):
@@ -465,16 +484,16 @@
     def do_cross(part, visitors, after):
         return cross(tie(owns[part], after), (*visitors, swapped[part]))
 
-    owns = [assemble(p0, 0)]
+    owns = assemble(p0)
     swapped = [swap(0)]
     chosen = choose(0)
     v0 = gather(0, chosen, None, None)
     a0 = outer(tie(owns[0], chosen), swapped[0])
     ya0 = exchange(tie(a0, p1), "yA0")
-    owns.append(assemble(tie(p1, chosen), 0))
+    owns += assemble(tie(p1, chosen))
     swapped.append(swap(1))
     p23 = transpose(spectra[2], ya0, "p23")
-    owns += [assemble(p23, 0), assemble(p23, 1)]
+    owns += assemble(p23)
     swapped += [swap(2), swap(3)]
     c0 = inner(owns[0], v0)
     y0 = exchange(tie(c0, p23), "y0")
@@ -486,8 +505,10 @@
     y2 = exchange(tie(c2, y1), "y2")
     v3 = gather(3, choose(3), v1, c2)
     c3 = do_cross(3, v3, (c2, y1))
-    y3 = exchange(tie(c3, y2), "y3")
-    return finish(y_arg, mask, mask0, ya0, y0, (y1, y2, y3)).reshape(32, 17, 32, 2, 128)
+    y3 = [lax.dynamic_index_in_dim(c3, (y + s) % 4, 0, keepdims=False) for s in range(4)]
+    with jax.named_scope("y3"):
+        y3 = [y3[0]] + [shift(y3[s], "y", s) for s in range(1, 4)]
+    return finish(y_arg, mask, mask0, ya0, y0, (y1, y2), y3).reshape(32, 17, 32, 2, 128)
 
 
 def solution(mesh):

time: 244 us -> 238 us (0.975); the launches traced: 240 us -> 236 us
  local copies, waits for them, and re-layouts: 9.18 us -> 11.9 us
  waiting for transfers between devices: 91.7 us -> 89.2 us
    all_to_all x5 -> x4, waiting for transfers between devices: 48.6 us -> 11 us  [exchange(): return lax.all_to_all(block, 'y', 0, 0, tiled=True)]
    ppermute x16 -> x19, waiting for transfers between devices: 36.5 us -> 71.6 us  [shift(): lax.ppermute(block, axis, [(i, (i + distance) % size) for i in range(size)])]
    all_to_all x5 -> x4, starting transfers between devices: 20.9 us -> 17.3 us  [exchange(): return lax.all_to_all(block, 'y', 0, 0, tiled=True)]
    ppermute x16 -> x19, starting transfers between devices: 14.3 us -> 17.8 us  [shift(): lax.ppermute(block, axis, [(i, (i + distance) % size) for i in range(size)])]
    squeeze x0 -> x1, local copies, waits for them, and re-layouts: none -> 2.6 us  [body(): lax.dynamic_index_in_dim(c3, (y + s) % 4, 0, keepdims=False)]
    pallas_call x4 -> x3, Pallas kernels: 6.58 us -> 4.88 us  [assemble(): pl.pallas_call(assemble_kernel, grid=(1,), in_specs=[whole(*pieces.shape)...]
    unnamed x38 -> x39, local copies, waits for them, and re-layouts: 6.85 us -> 6.22 us
  transfers between devices with their start and end apart: 26 -> 28, of which waited for: 13 -> 13; matrix products, arithmetic and copies ran while one was open for 4% -> 5% of each run, Pallas kernels for 16% -> 15%
where the time goes in v1:
time: 238 us; the launch traced here: 236 us
  waiting for transfers between devices  89.2 us (37%)
  Pallas kernels  56.1 us (24%)
  starting transfers between devices  53.6 us (23%)
  blocking collectives  17.7 us (7%)
  local copies, waits for them, and re-layouts  11.9 us (5%)
  other arithmetic  7.47 us (3%)
    ppermute x19, waiting for transfers between devices, shift(): lax.ppermute(block, axis, [(i, (i + distance) % size) for i in range(size)])  71.6 us
    pallas_call x3, Pallas kernels, cross(): pl.pallas_call(cross_kernel, grid=(1,), in_specs=[whole(NF, 128, 256) for...  18.9 us
    ppermute x19, starting transfers between devices, shift(): lax.ppermute(block, axis, [(i, (i + distance) % size) for i in range(size)])  17.8 us
    all_to_all x1, blocking collectives, transpose(): lax.all_to_all(tie(block, after), ('zh', 'core', 'y'), 0, 0, tiled=True)  17.7 us
    all_to_all x4, starting transfers between devices, exchange(): return lax.all_to_all(block, 'y', 0, 0, tiled=True)  17.3 us
    all_to_all x2, starting transfers between devices, transpose(): lax.all_to_all(tie(block, after), ('zh', 'core', 'y'), 0, 0, tiled=True)  13.1 us
    all_to_all x4, waiting for transfers between devices, exchange(): return lax.all_to_all(block, 'y', 0, 0, tiled=True)  11 us
    pallas_call x1, Pallas kernels, finish(): pl.pallas_call(finish_kernel, grid_spec=pltpu.PrefetchScalarGridSpec(num_...  10.9 us
  transfers between devices with their start and end apart: 28, of which 13 were waited for; matrix products, arithmetic and copies ran while one was open for 5% of the time, Pallas kernels for 15%

profile of v1, /device:TPU:1, one launch (start us, length us, event | category | flops | bytes accessed | tf_op | source)
XLA Modules:
  0.0 236.4 jit_solution(17882745173818911740)
XLA Ops:
  1.3 5.0 %collective-permute-start.2 = (f32[8]{0:T(128)}, f32[8]{0:T(128)}, u32[]{:S(2)}, u32[]{:S(2)}) collective-permute-start(f32[8]{0:T(128)} %convert_reduce_fusion), channel_id=1, source_target_pairs={{0,3},{1,2},{2,1},{3,0},{4,7},{5,6},{6,5},{7,4},{8,11},{9,10},{10,... | collective-permute-start | bytes 104 | tf_op jit(solution)/shard_map/ppermute | solution.py:442
  11.2 4.6 %normalize.1.x_ref = bf16[1024,1024]{1,0:T(8,128)(2,1)S(1)} custom-call(bf16[1024,1024]{1,0:T(8,128)(2,1)S(1)} %bitcast.16, s32[32,4]{1,0:T(8,128)S(1)} %copy.28.starts_ref, s32[32,1]{1,0:T(8,128)S(1)} %copy.29.counts_ref, bf16[1024,1024]{1,0:T(8,128)(2,1)} %constant.88.clone.band_ref, f32[1,1024]{1,0:T(1,128)S(1)} %copy-done.5, f32[1,1024]{1,0:T(1,128)S(1)} %copy-done.4), custom_call_target="tpu_custom_call" | custom-call | flops 206999994368 | bytes 648000000 | tf_op jit(solution)/shard_map/normalize/pallas_call | solution.py:89
  16.7 8.7 %whiten.1 = (bf16[16,8,16,128]{3,2,1,0:T(8,128)(2,1)S(1)}, bf16[16,8,16,128]{3,2,1,0:T(8,128)(2,1)}, bf16[16,16,16,128]{3,2,1,0:T(8,128)(2,1)}) custom-call(bf16[1024,1024]{1,0:T(8,128)(2,1)S(1)} %normalize.1.x_ref, f32[1,1024]{1,0:T(1,128)S(1)} %broadcast_in_dim_reshape.3.root_ref, bf16[1024,1024]{1,0:T(8,128)(2,1)} %constant.91.clone.dft_ref, ...), custom_call_target="tpu_custom_call" | custom-call | flops 310499999744 | bytes 972000000 | tf_op jit(solution)/shard_map/whiten/pallas_call | solution.py:144
  25.4 17.7 %all_to_all.35.piece_ref = bf16[16,8,16,128]{3,2,1,0:T(8,128)(2,1)S(1)} all-to-all(bf16[16,8,16,128]{3,2,1,0:T(8,128)(2,1)S(1)} %get-tuple-element.40), channel_id=1, replica_groups=mesh['zl'=2,'x'=4,'y'=4,'zh'=2,'core'=2] {'zh','core','y'}, dimensions={0} | all-to-all | bytes 1048576 | tf_op jit(solution)/shard_map/p0/all_to_all | solution.py:462
  44.5 5.5 %all-to-all-start.1 = ((bf16[16,8,16,128]{3,2,1,0:T(8,128)(2,1)}), bf16[16,8,16,128]{3,2,1,0:T(8,128)(2,1)S(1)}, u32[]{:S(2)}, u32[]{:S(2)}) async-start(bf16[16,8,16,128]{3,2,1,0:T(8,128)(2,1)} %get-tuple-element.46), calls=%async_computation.1 | async-start | bytes 1048576 | tf_op jit(solution)/shard_map/p1/all_to_all | solution.py:462
  50.0 9.8 %collective-permute-done.3.v4_ref = bf16[8,128,256]{2,1,0:T(8,128)(2,1)S(1)} collective-permute-done((bf16[8,128,256]{2,1,0:T(8,128)(2,1)S(1)}, bf16[8,128,256]{2,1,0:T(8,128)(2,1)S(1)}, u32[]{:S(2)}, u32[]{:S(2)}) %collective-permute-start.3) | collective-permute-done | bytes 524320 | tf_op jit(solution)/shard_map/z0/ppermute | solution.py:431
  59.9 2.5 %collective-permute-start.4 = (bf16[8,128,256]{2,1,0:T(8,128)(2,1)S(1)}, bf16[8,128,256]{2,1,0:T(8,128)(2,1)}, u32[]{:S(2)}, u32[]{:S(2)}) collective-permute-start(bf16[8,128,256]{2,1,0:T(8,128)(2,1)S(1)} %get-tuple-element.41), channel_id=1, source_target_pairs={{0,48},{16,0},{32,16},{48,32},{1,49},{17,1},{33,17},{49,33},{2,50}... | collective-permute-start | bytes 1572872 | tf_op jit(solution)/shard_map/x0/ppermute | solution.py:431
  64.6 3.4 %outer.1 = bf16[4,320,256]{2,1,0:T(8,128)(2,1)} custom-call(bf16[8,128,256]{2,1,0:T(8,128)(2,1)} %copy-done, bf16[8,128,256]{2,1,0:T(8,128)(2,1)} %copy-done.8, bf16[256,512]{1,0:T(8,128)(2,1)} %constant.94.clone.spread_ref), custom_call_target="tpu_custom_call" | custom-call | flops 103499997184 | bytes 324000000 | tf_op jit(solution)/shard_map/outer/pallas_call | solution.py:320
  68.0 3.7 %all-to-all-start.2 = ((bf16[4,320,256]{2,1,0:T(8,128)(2,1)}), bf16[4,320,256]{2,1,0:T(8,128)(2,1)S(1)}, u32[]{:S(2)}, u32[]{:S(2)}) async-start(bf16[4,320,256]{2,1,0:T(8,128)(2,1)} %outer.1), calls=%async_computation.2 | async-start | bytes 1310720 | tf_op jit(solution)/shard_map/yA0/all_to_all | solution.py:474
  73.8 6.2 %all-to-all-done.2.outer_ref.outer0_ref = bf16[4,320,256]{2,1,0:T(8,128)(2,1)S(1)} async-done(((bf16[4,320,256]{2,1,0:T(8,128)(2,1)}), bf16[4,320,256]{2,1,0:T(8,128)(2,1)S(1)}, u32[]{:S(2)}, u32[]{:S(2)}) %all-to-all-start.2) | async-done | bytes 655392 | tf_op jit(solution)/shard_map/yA0/all_to_all | solution.py:474
  80.0 7.7 %all-to-all-start.3 = ((bf16[16,16,16,128]{3,2,1,0:T(8,128)(2,1)}), bf16[16,16,16,128]{3,2,1,0:T(8,128)(2,1)}, u32[]{:S(2)}, u32[]{:S(2)}) async-start(bf16[16,16,16,128]{3,2,1,0:T(8,128)(2,1)} %get-tuple-element.49), calls=%async_computation.3 | async-start | bytes 2097152 | tf_op jit(solution)/shard_map/p23/all_to_all | solution.py:462
  89.1 4.7 %inner.1 = bf16[4,256,768]{2,1,0:T(8,128)(2,1)} custom-call(bf16[8,128,256]{2,1,0:T(8,128)(2,1)} %copy-done, bf16[8,128,256]{2,1,0:T(8,128)(2,1)} %collective-permute-done.4.v1_ref, bf16[8,128,256]{2,1,0:T(8,128)(2,1)} %collective-permute-done.5.v2_ref, bf16[8,128,256]{2,1,0:T(8,128)(2,1)} %collective-permute-done.6.v3_ref, ...), custom_call_target="tpu_custom_call" | custom-call | flops 172499992576 | bytes 540000000 | tf_op jit(solution)/shard_map/inner/pallas_call | solution.py:320
  97.8 5.5 %all-to-all-done.3.piece_ref = bf16[16,16,16,128]{3,2,1,0:T(8,128)(2,1)} async-done(((bf16[16,16,16,128]{3,2,1,0:T(8,128)(2,1)}), bf16[16,16,16,128]{3,2,1,0:T(8,128)(2,1)}, u32[]{:S(2)}, u32[]{:S(2)}) %all-to-all-start.3) | async-done | bytes 1048608 | tf_op jit(solution)/shard_map/p23/all_to_all | solution.py:462
  103.3 3.0 %assemble.5 = (bf16[8,128,256]{2,1,0:T(8,128)(2,1)}, bf16[8,128,256]{2,1,0:T(8,128)(2,1)}) custom-call(bf16[16,16,16,128]{3,2,1,0:T(8,128)(2,1)} %all-to-all-done.3.piece_ref), custom_call_target="tpu_custom_call" | custom-call | flops 55199997952 | bytes 172800000 | tf_op jit(solution)/shard_map/assemble/pallas_call | solution.py:200
  107.8 4.3 %all-to-all-start.4 = ((bf16[4,256,768]{2,1,0:T(8,128)(2,1)}), bf16[4,256,768]{2,1,0:T(8,128)(2,1)}, u32[]{:S(2)}, u32[]{:S(2)}) async-start(bf16[4,256,768]{2,1,0:T(8,128)(2,1)} %inner.1), calls=%async_computation.4 | async-start | bytes 3145728 | tf_op jit(solution)/shard_map/y0/all_to_all | solution.py:474
  112.1 7.5 %collective-permute-done.8.v1_ref = bf16[8,128,256]{2,1,0:T(8,128)(2,1)S(1)} collective-permute-done((bf16[8,128,256]{2,1,0:T(8,128)(2,1)S(1)}, bf16[8,128,256]{2,1,0:T(8,128)(2,1)S(1)}, u32[]{:S(2)}, u32[]{:S(2)}) %collective-permute-start.8) | collective-permute-done | bytes 524320 | tf_op jit(solution)/shard_map/x1/ppermute | solution.py:431
  119.6 2.3 collective-permute-done.10.v3_ref
  122.7 6.3 %cross.3 = bf16[4,272,1024]{2,1,0:T(8,128)(2,1)} custom-call(bf16[8,128,256]{2,1,0:T(8,128)(2,1)} %assemble.4.own_ref, bf16[8,128,256]{2,1,0:T(8,128)(2,1)} %copy-done.16, bf16[8,128,256]{2,1,0:T(8,128)(2,1)} %copy-done.14, bf16[8,128,256]{2,1,0:T(8,128)(2,1)} %copy-done.17, bf16[8,128,256]{2,1,0:T(8,128)(2,1)} %collective-permute-done.7.v4_ref, ...), custom_call_target="tpu_custom_call" | custom-call | flops 344999985152 | bytes 1080000000 | tf_op jit(solution)/shard_map/cross/pallas_call | solution.py:256
  133.2 2.5 %broadcast_select_fusion = (bf16[8,128,256]{2,1,0:T(8,128)(2,1)}, bf16[8,128,256]{2,1,0:T(8,128)(2,1)}, bf16[8,128,256]{2,1,0:T(8,128)(2,1)}) fusion(bf16[8,128,256]{2,1,0:T(8,128)(2,1)} %collective-permute-done.15.v4_ref, bf16[8,128,256]{2,1,0:T(8,128)(2,1)} %get-tuple-element.68.own_ref, pred[]{:T(512)S(6)} %lt.65, pred[]{:T(512)S(6)} %lt.64, pred[]{:T(512)S(6)} %lt.63), kind=kLoop, calls=%fused_computation.7 | loop fusion | flops 786432 | bytes 2621443 | tf_op jit(solution)/shard_map/x3/jit(_where)/select_n | solution.py:478
  137.2 4.7 %all-to-all-start.5 = ((bf16[4,272,1024]{2,1,0:T(8,128)(2,1)}), bf16[4,272,1024]{2,1,0:T(8,128)(2,1)}, u32[]{:S(2)}, u32[]{:S(2)}) async-start(bf16[4,272,1024]{2,1,0:T(8,128)(2,1)} %cross.3), calls=%async_computation.5 | async-start | bytes 4456448 | tf_op jit(solution)/shard_map/y1/all_to_all | solution.py:474
  141.9 2.8 %collective-permute-done.14.v3_ref = bf16[8,128,256]{2,1,0:T(8,128)(2,1)S(1)} collective-permute-done((bf16[8,128,256]{2,1,0:T(8,128)(2,1)S(1)}, bf16[8,128,256]{2,1,0:T(8,128)(2,1)S(1)}, u32[]{:S(2)}, u32[]{:S(2)}) %collective-permute-start.14) | collective-permute-done | bytes 524320 | tf_op jit(solution)/shard_map/x2/ppermute | solution.py:431
  144.7 11.4 %collective-permute-done.13.v2_ref = bf16[8,128,256]{2,1,0:T(8,128)(2,1)S(1)} collective-permute-done((bf16[8,128,256]{2,1,0:T(8,128)(2,1)S(1)}, bf16[8,128,256]{2,1,0:T(8,128)(2,1)S(1)}, u32[]{:S(2)}, u32[]{:S(2)}) %collective-permute-start.13) | collective-permute-done | bytes 524320 | tf_op jit(solution)/shard_map/x2/ppermute | solution.py:431
  157.0 6.4 %cross.4 = bf16[4,272,1024]{2,1,0:T(8,128)(2,1)} custom-call(bf16[8,128,256]{2,1,0:T(8,128)(2,1)} %get-tuple-element.60.own_ref, bf16[8,128,256]{2,1,0:T(8,128)(2,1)} %copy-done.13, bf16[8,128,256]{2,1,0:T(8,128)(2,1)} %copy-done.15, bf16[8,128,256]{2,1,0:T(8,128)(2,1)} %copy-done.12, bf16[8,128,256]{2,1,0:T(8,128)(2,1)} %collective-permute-done.11.v4_ref, ...), custom_call_target="tpu_custom_call" | custom-call | flops 344999985152 | bytes 1080000000 | tf_op jit(solution)/shard_map/cross/pallas_call | solution.py:256
  163.8 4.8 %all-to-all-done.5.rest_0_.rest_2_ = bf16[4,272,1024]{2,1,0:T(8,128)(2,1)} async-done(((bf16[4,272,1024]{2,1,0:T(8,128)(2,1)}), bf16[4,272,1024]{2,1,0:T(8,128)(2,1)}, u32[]{:S(2)}, u32[]{:S(2)}) %all-to-all-start.5) | async-done | bytes 2228256 | tf_op jit(solution)/shard_map/y1/all_to_all | solution.py:474
  168.7 4.5 %all-to-all-start.6 = ((bf16[4,272,1024]{2,1,0:T(8,128)(2,1)}), bf16[4,272,1024]{2,1,0:T(8,128)(2,1)}, u32[]{:S(2)}, u32[]{:S(2)}) async-start(bf16[4,272,1024]{2,1,0:T(8,128)(2,1)} %cross.4), calls=%async_computation.6 | async-start | bytes 4456448 | tf_op jit(solution)/shard_map/y2/all_to_all | solution.py:474
  173.2 3.5 %collective-permute-done.17.v2_ref = bf16[8,128,256]{2,1,0:T(8,128)(2,1)S(1)} collective-permute-done((bf16[8,128,256]{2,1,0:T(8,128)(2,1)S(1)}, bf16[8,128,256]{2,1,0:T(8,128)(2,1)S(1)}, u32[]{:S(2)}, u32[]{:S(2)}) %collective-permute-start.17) | collective-permute-done | bytes 524320 | tf_op jit(solution)/shard_map/x3/ppermute | solution.py:431
  177.5 6.3 %cross.5 = bf16[4,272,1024]{2,1,0:T(8,128)(2,1)} custom-call(bf16[8,128,256]{2,1,0:T(8,128)(2,1)} %get-tuple-element.68.own_ref, bf16[8,128,256]{2,1,0:T(8,128)(2,1)} %collective-permute-done.16.v1_ref, bf16[8,128,256]{2,1,0:T(8,128)(2,1)} %copy-done.11, bf16[8,128,256]{2,1,0:T(8,128)(2,1)} %collective-permute-done.18.v3_ref, ...), custom_call_target="tpu_custom_call" | custom-call | flops 344999985152 | bytes 1080000000 | tf_op jit(solution)/shard_map/cross/pallas_call | solution.py:256
  183.8 2.6 %dynamic-slice_bitcast_fusion = (bf16[272,1024]{1,0:T(8,128)(2,1)S(1)}, bf16[272,1024]{1,0:T(8,128)(2,1)S(1)}, bf16[272,1024]{1,0:T(8,128)(2,1)S(1)}, bf16[272,1024]{1,0:T(8,128)(2,1)}) fusion(bf16[4,272,1024]{2,1,0:T(8,128)(2,1)} %cross.5, s32[]{:T(128)S(6)} %select_n.124, s32[]{:T(128)S(6)} %select_n.122, s32[]{:T(128)S(6)} %select_n.120, s32[]{:T(128)S(6)} %select_n.118), kind=kLoop, calls=%fused_computation.2 | loop fusion | bytes 4456464 | tf_op jit(solution)/shard_map/jit(dynamic_index_in_dim)/squeeze | solution.py:508
  186.4 2.3 collective-permute-start.21
  192.4 19.2 %collective-permute-done.21.rest_7_.rest_11_ = bf16[272,1024]{1,0:T(8,128)(2,1)S(1)} collective-permute-done((bf16[272,1024]{1,0:T(8,128)(2,1)S(1)}, bf16[272,1024]{1,0:T(8,128)(2,1)S(1)}, u32[]{:S(2)}, u32[]{:S(2)}) %collective-permute-start.21) | collective-permute-done | bytes 557088 | tf_op jit(solution)/shard_map/y3/ppermute | solution.py:431
  211.6 13.7 %collective-permute-done.19.rest_5_.rest_9_ = bf16[272,1024]{1,0:T(8,128)(2,1)} collective-permute-done((bf16[272,1024]{1,0:T(8,128)(2,1)S(1)}, bf16[272,1024]{1,0:T(8,128)(2,1)}, u32[]{:S(2)}, u32[]{:S(2)}) %collective-permute-start.19) | collective-permute-done | bytes 557088 | tf_op jit(solution)/shard_map/y3/ppermute | solution.py:431
  225.3 10.9 %finish.1 = bf16[34816,128]{1,0:T(8,128)(2,1)} custom-call(s32[1]{0:T(128)} %bitcast.y_ref, f32[8,4,1024]{2,1,0:T(4,128)} %reshape.14.mask_ref, f32[16,1,128]{2,1,0:T(1,128)} %reshape_squeeze.3.mask0_ref, bf16[4,320,256]{2,1,0:T(8,128)(2,1)} %copy-done.6, bf16[4,320,256]{2,1,0:T(8,128)(2,1)} %copy-done.6, bf16[4,256,768]{2,1,0:T(8,128)(2,1)} %all-to-all-done.4.inner_ref, ...), custom_call_target="tpu_custom_call" | custom-call | flops 310499999744 | bytes 972000000 | tf_op jit(solution)/shard_map/finish/pallas_call | solution.py:398
  (97 shorter events, 32.0 us)
Async XLA Ops:
  1.3 14.5 %collective-permute-start.2 = (f32[8]{0:T(128)}, f32[8]{0:T(128)}, u32[]{:S(2)}, u32[]{:S(2)}) collective-permute-start(f32[8]{0:T(128)} %convert_reduce_fusion), channel_id=1, source_target_pairs={{0,3},{1,2},{2,1},{3,0},{4,7},{5,6},{6,5},{7,4},{8,11},{9,10},{10,... | collective-permute-start | bytes 104 | tf_op jit(solution)/shard_map/ppermute | solution.py:442
  6.3 9.5 %collective-permute-start.1 = (f32[8]{0:T(128)}, f32[8]{0:T(128)}, u32[]{:S(2)}, u32[]{:S(2)}) collective-permute-start(f32[8]{0:T(128)} %convert_reduce_fusion), channel_id=1, source_target_pairs={{0,2},{1,3},{2,0},{3,1},{4,6},{5,7},{6,4},{7,5},{8,10},{9,11},{10,... | collective-permute-start | bytes 104 | tf_op jit(solution)/shard_map/ppermute | solution.py:442
  6.3 9.5 %collective-permute-start = (f32[8]{0:T(128)}, f32[8]{0:T(128)}, u32[]{:S(2)}, u32[]{:S(2)}) collective-permute-start(f32[8]{0:T(128)} %convert_reduce_fusion), channel_id=1, source_target_pairs={{0,1},{1,0},{2,3},{3,2},{4,5},{5,4},{6,7},{7,6},{8,9},{9,8},{10,11... | collective-permute-start | bytes 104 | tf_op jit(solution)/shard_map/ppermute | solution.py:442
  43.7 20.9 %copy-start = (bf16[8,128,256]{2,1,0:T(8,128)(2,1)}, bf16[8,128,256]{2,1,0:T(8,128)(2,1)S(1)}, u32[]{:S(2)}) copy-start(bf16[8,128,256]{2,1,0:T(8,128)(2,1)S(1)} %assemble.3.own_ref) | copy-start | bytes 1572868
  43.7 16.1 %collective-permute-start.3 = (bf16[8,128,256]{2,1,0:T(8,128)(2,1)S(1)}, bf16[8,128,256]{2,1,0:T(8,128)(2,1)S(1)}, u32[]{:S(2)}, u32[]{:S(2)}) collective-permute-start(bf16[8,128,256]{2,1,0:T(8,128)(2,1)S(1)} %assemble.3.own_ref), channel_id=1, source_target_pairs={{0,64},{64,0},{1,65},{65,1},{2,66},{66,2},{3,67},{67,3},{4,68},{68... | collective-permute-start | bytes 1572872 | tf_op jit(solution)/shard_map/z0/ppermute | solution.py:431
  44.5 20.1 %all-to-all-start.1 = ((bf16[16,8,16,128]{3,2,1,0:T(8,128)(2,1)}), bf16[16,8,16,128]{3,2,1,0:T(8,128)(2,1)S(1)}, u32[]{:S(2)}, u32[]{:S(2)}) async-start(bf16[16,8,16,128]{3,2,1,0:T(8,128)(2,1)} %get-tuple-element.46), calls=%async_computation.1 | async-start | bytes 1048576 | tf_op jit(solution)/shard_map/p1/all_to_all | solution.py:462
  59.9 27.8 %collective-permute-start.4 = (bf16[8,128,256]{2,1,0:T(8,128)(2,1)S(1)}, bf16[8,128,256]{2,1,0:T(8,128)(2,1)}, u32[]{:S(2)}, u32[]{:S(2)}) collective-permute-start(bf16[8,128,256]{2,1,0:T(8,128)(2,1)S(1)} %get-tuple-element.41), channel_id=1, source_target_pairs={{0,48},{16,0},{32,16},{48,32},{1,49},{17,1},{33,17},{49,33},{2,50}... | collective-permute-start | bytes 1572872 | tf_op jit(solution)/shard_map/x0/ppermute | solution.py:431
  62.4 25.2 %collective-permute-start.5 = (bf16[8,128,256]{2,1,0:T(8,128)(2,1)S(1)}, bf16[8,128,256]{2,1,0:T(8,128)(2,1)}, u32[]{:S(2)}, u32[]{:S(2)}) collective-permute-start(bf16[8,128,256]{2,1,0:T(8,128)(2,1)S(1)} %get-tuple-element.42), channel_id=1, source_target_pairs={{0,32},{16,48},{32,0},{48,16},{1,33},{17,49},{33,1},{49,17},{2,34}... | collective-permute-start | bytes 1572872 | tf_op jit(solution)/shard_map/x0/ppermute | solution.py:431
  63.0 26.1 %collective-permute-start.6 = (bf16[8,128,256]{2,1,0:T(8,128)(2,1)S(1)}, bf16[8,128,256]{2,1,0:T(8,128)(2,1)}, u32[]{:S(2)}, u32[]{:S(2)}) collective-permute-start(bf16[8,128,256]{2,1,0:T(8,128)(2,1)S(1)} %get-tuple-element.43), channel_id=1, source_target_pairs={{0,16},{16,32},{32,48},{48,0},{1,17},{17,33},{33,49},{49,1},{2,18}... | collective-permute-start | bytes 1572872 | tf_op jit(solution)/shard_map/x0/ppermute | solution.py:431
  68.0 12.0 %all-to-all-start.2 = ((bf16[4,320,256]{2,1,0:T(8,128)(2,1)}), bf16[4,320,256]{2,1,0:T(8,128)(2,1)S(1)}, u32[]{:S(2)}, u32[]{:S(2)}) async-start(bf16[4,320,256]{2,1,0:T(8,128)(2,1)} %outer.1), calls=%async_computation.2 | async-start | bytes 1310720 | tf_op jit(solution)/shard_map/yA0/all_to_all | solution.py:474
  73.1 20.8 %collective-permute-start.7 = (bf16[8,128,256]{2,1,0:T(8,128)(2,1)}, bf16[8,128,256]{2,1,0:T(8,128)(2,1)}, u32[]{:S(2)}, u32[]{:S(2)}) collective-permute-start(bf16[8,128,256]{2,1,0:T(8,128)(2,1)} %assemble.4.own_ref), channel_id=1, source_target_pairs={{0,64},{64,0},{1,65},{65,1},{2,66},{66,2},{3,67},{67,3},{4,68},{68... | collective-permute-start | bytes 1572872 | tf_op jit(solution)/shard_map/z1/ppermute | solution.py:431
  80.0 13.9 %copy-start.6 = (bf16[4,320,256]{2,1,0:T(8,128)(2,1)}, bf16[4,320,256]{2,1,0:T(8,128)(2,1)S(1)}, u32[]{:S(2)}) copy-start(bf16[4,320,256]{2,1,0:T(8,128)(2,1)S(1)} %all-to-all-done.2.outer_ref.outer0_ref) | copy-start | bytes 1966084
  80.0 23.3 %all-to-all-start.3 = ((bf16[16,16,16,128]{3,2,1,0:T(8,128)(2,1)}), bf16[16,16,16,128]{3,2,1,0:T(8,128)(2,1)}, u32[]{:S(2)}, u32[]{:S(2)}) async-start(bf16[16,16,16,128]{3,2,1,0:T(8,128)(2,1)} %get-tuple-element.49), calls=%async_computation.3 | async-start | bytes 2097152 | tf_op jit(solution)/shard_map/p23/all_to_all | solution.py:462
  95.2 16.9 %collective-permute-start.9 = (bf16[8,128,256]{2,1,0:T(8,128)(2,1)S(1)}, bf16[8,128,256]{2,1,0:T(8,128)(2,1)S(1)}, u32[]{:S(2)}, u32[]{:S(2)}) collective-permute-start(bf16[8,128,256]{2,1,0:T(8,128)(2,1)S(1)} %get-tuple-element.57), channel_id=1, source_target_pairs={{0,32},{16,48},{32,0},{48,16},{1,33},{17,49},{33,1},{49,17},{2,34}... | collective-permute-start | bytes 1572872 | tf_op jit(solution)/shard_map/x1/ppermute | solution.py:431
  96.3 23.3 %collective-permute-start.8 = (bf16[8,128,256]{2,1,0:T(8,128)(2,1)S(1)}, bf16[8,128,256]{2,1,0:T(8,128)(2,1)S(1)}, u32[]{:S(2)}, u32[]{:S(2)}) collective-permute-start(bf16[8,128,256]{2,1,0:T(8,128)(2,1)S(1)} %get-tuple-element.55), channel_id=1, source_target_pairs={{0,48},{16,0},{32,16},{48,32},{1,49},{17,1},{33,17},{49,33},{2,50}... | collective-permute-start | bytes 1572872 | tf_op jit(solution)/shard_map/x1/ppermute | solution.py:431
  97.7 24.2 %collective-permute-start.10 = (bf16[8,128,256]{2,1,0:T(8,128)(2,1)S(1)}, bf16[8,128,256]{2,1,0:T(8,128)(2,1)S(1)}, u32[]{:S(2)}, u32[]{:S(2)}) collective-permute-start(bf16[8,128,256]{2,1,0:T(8,128)(2,1)S(1)} %get-tuple-element.58), channel_id=1, source_target_pairs={{0,16},{16,32},{32,48},{48,0},{1,17},{17,33},{33,49},{49,1},{2,18}... | collective-permute-start | bytes 1572872 | tf_op jit(solution)/shard_map/x1/ppermute | solution.py:431
  106.3 22.8 %collective-permute-start.11 = (bf16[8,128,256]{2,1,0:T(8,128)(2,1)}, bf16[8,128,256]{2,1,0:T(8,128)(2,1)}, u32[]{:S(2)}, u32[]{:S(2)}) collective-permute-start(bf16[8,128,256]{2,1,0:T(8,128)(2,1)} %get-tuple-element.60.own_ref), channel_id=1, source_target_pairs={{0,64},{64,0},{1,65},{65,1},{2,66},{66,2},{3,67},{67,3},{4,68},{68... | collective-permute-start | bytes 1572872 | tf_op jit(solution)/shard_map/z2/ppermute | solution.py:431
  107.1 26.1 %collective-permute-start.15 = (bf16[8,128,256]{2,1,0:T(8,128)(2,1)}, bf16[8,128,256]{2,1,0:T(8,128)(2,1)}, u32[]{:S(2)}, u32[]{:S(2)}) collective-permute-start(bf16[8,128,256]{2,1,0:T(8,128)(2,1)} %get-tuple-element.68.own_ref), channel_id=1, source_target_pairs={{0,64},{64,0},{1,65},{65,1},{2,66},{66,2},{3,67},{67,3},{4,68},{68... | collective-permute-start | bytes 1572872 | tf_op jit(solution)/shard_map/z3/ppermute | solution.py:431
  107.8 29.5 %all-to-all-start.4 = ((bf16[4,256,768]{2,1,0:T(8,128)(2,1)}), bf16[4,256,768]{2,1,0:T(8,128)(2,1)}, u32[]{:S(2)}, u32[]{:S(2)}) async-start(bf16[4,256,768]{2,1,0:T(8,128)(2,1)} %inner.1), calls=%async_computation.4 | async-start | bytes 3145728 | tf_op jit(solution)/shard_map/y0/all_to_all | solution.py:474
  130.3 14.4 %collective-permute-start.14 = (bf16[8,128,256]{2,1,0:T(8,128)(2,1)S(1)}, bf16[8,128,256]{2,1,0:T(8,128)(2,1)S(1)}, u32[]{:S(2)}, u32[]{:S(2)}) collective-permute-start(bf16[8,128,256]{2,1,0:T(8,128)(2,1)S(1)} %get-tuple-element.66), channel_id=1, source_target_pairs={{0,16},{16,32},{32,48},{48,0},{1,17},{17,33},{33,49},{49,1},{2,18}... | collective-permute-start | bytes 1572872 | tf_op jit(solution)/shard_map/x2/ppermute | solution.py:431
  130.8 13.9 %collective-permute-start.12 = (bf16[8,128,256]{2,1,0:T(8,128)(2,1)S(1)}, bf16[8,128,256]{2,1,0:T(8,128)(2,1)S(1)}, u32[]{:S(2)}, u32[]{:S(2)}) collective-permute-start(bf16[8,128,256]{2,1,0:T(8,128)(2,1)S(1)} %get-tuple-element.62), channel_id=1, source_target_pairs={{0,48},{16,0},{32,16},{48,32},{1,49},{17,1},{33,17},{49,33},{2,50}... | collective-permute-start | bytes 1572872 | tf_op jit(solution)/shard_map/x2/ppermute | solution.py:431
  133.1 23.0 %collective-permute-start.13 = (bf16[8,128,256]{2,1,0:T(8,128)(2,1)S(1)}, bf16[8,128,256]{2,1,0:T(8,128)(2,1)S(1)}, u32[]{:S(2)}, u32[]{:S(2)}) collective-permute-start(bf16[8,128,256]{2,1,0:T(8,128)(2,1)S(1)} %get-tuple-element.64), channel_id=1, source_target_pairs={{0,32},{16,48},{32,0},{48,16},{1,33},{17,49},{33,1},{49,17},{2,34}... | collective-permute-start | bytes 1572872 | tf_op jit(solution)/shard_map/x2/ppermute | solution.py:431
  135.7 37.5 %collective-permute-start.16 = (bf16[8,128,256]{2,1,0:T(8,128)(2,1)}, bf16[8,128,256]{2,1,0:T(8,128)(2,1)}, u32[]{:S(2)}, u32[]{:S(2)}) collective-permute-start(bf16[8,128,256]{2,1,0:T(8,128)(2,1)} %get-tuple-element.70), channel_id=1, source_target_pairs={{0,48},{16,0},{32,16},{48,32},{1,49},{17,1},{33,17},{49,33},{2,50}... | collective-permute-start | bytes 1572872 | tf_op jit(solution)/shard_map/x3/ppermute | solution.py:431
  137.2 36.0 %collective-permute-start.18 = (bf16[8,128,256]{2,1,0:T(8,128)(2,1)}, bf16[8,128,256]{2,1,0:T(8,128)(2,1)}, u32[]{:S(2)}, u32[]{:S(2)}) collective-permute-start(bf16[8,128,256]{2,1,0:T(8,128)(2,1)} %get-tuple-element.74), channel_id=1, source_target_pairs={{0,16},{16,32},{32,48},{48,0},{1,17},{17,33},{33,49},{49,1},{2,18}... | collective-permute-start | bytes 1572872 | tf_op jit(solution)/shard_map/x3/ppermute | solution.py:431
  137.2 31.4 %all-to-all-start.5 = ((bf16[4,272,1024]{2,1,0:T(8,128)(2,1)}), bf16[4,272,1024]{2,1,0:T(8,128)(2,1)}, u32[]{:S(2)}, u32[]{:S(2)}) async-start(bf16[4,272,1024]{2,1,0:T(8,128)(2,1)} %cross.3), calls=%async_computation.5 | async-start | bytes 4456448 | tf_op jit(solution)/shard_map/y1/all_to_all | solution.py:474
  144.7 11.4 %copy-start.12 = (bf16[8,128,256]{2,1,0:T(8,128)(2,1)}, bf16[8,128,256]{2,1,0:T(8,128)(2,1)S(1)}, u32[]{:S(2)}) copy-start(bf16[8,128,256]{2,1,0:T(8,128)(2,1)S(1)} %collective-permute-done.14.v3_ref) | copy-start | bytes 1572868
  163.3 13.4 %collective-permute-start.17 = (bf16[8,128,256]{2,1,0:T(8,128)(2,1)S(1)}, bf16[8,128,256]{2,1,0:T(8,128)(2,1)S(1)}, u32[]{:S(2)}, u32[]{:S(2)}) collective-permute-start(bf16[8,128,256]{2,1,0:T(8,128)(2,1)S(1)} %copy-done.7), channel_id=1, source_target_pairs={{0,32},{16,48},{32,0},{48,16},{1,33},{17,49},{33,1},{49,17},{2,34}... | collective-permute-start | bytes 1572872 | tf_op jit(solution)/shard_map/x3/ppermute | solution.py:431
  168.7 56.6 %all-to-all-start.6 = ((bf16[4,272,1024]{2,1,0:T(8,128)(2,1)}), bf16[4,272,1024]{2,1,0:T(8,128)(2,1)}, u32[]{:S(2)}, u32[]{:S(2)}) async-start(bf16[4,272,1024]{2,1,0:T(8,128)(2,1)} %cross.4), calls=%async_computation.6 | async-start | bytes 4456448 | tf_op jit(solution)/shard_map/y2/all_to_all | solution.py:474
  186.4 25.2 %collective-permute-start.21 = (bf16[272,1024]{1,0:T(8,128)(2,1)S(1)}, bf16[272,1024]{1,0:T(8,128)(2,1)S(1)}, u32[]{:S(2)}, u32[]{:S(2)}) collective-permute-start(bf16[272,1024]{1,0:T(8,128)(2,1)S(1)} %get-tuple-element.75), channel_id=1, source_target_pairs={{0,12},{4,0},{8,4},{12,8},{1,13},{5,1},{9,5},{13,9},{2,14},{6,2},{... | collective-permute-start | bytes 1671176 | tf_op jit(solution)/shard_map/y3/ppermute | solution.py:431
  188.7 22.9 %collective-permute-start.20 = (bf16[272,1024]{1,0:T(8,128)(2,1)S(1)}, bf16[272,1024]{1,0:T(8,128)(2,1)}, u32[]{:S(2)}, u32[]{:S(2)}) collective-permute-start(bf16[272,1024]{1,0:T(8,128)(2,1)S(1)} %get-tuple-element.76), channel_id=1, source_target_pairs={{0,8},{4,12},{8,0},{12,4},{1,9},{5,13},{9,1},{13,5},{2,10},{6,14},... | collective-permute-start | bytes 1671176 | tf_op jit(solution)/shard_map/y3/ppermute | solution.py:431
  190.1 35.2 %collective-permute-start.19 = (bf16[272,1024]{1,0:T(8,128)(2,1)S(1)}, bf16[272,1024]{1,0:T(8,128)(2,1)}, u32[]{:S(2)}, u32[]{:S(2)}) collective-permute-start(bf16[272,1024]{1,0:T(8,128)(2,1)S(1)} %get-tuple-element.77), channel_id=1, source_target_pairs={{0,4},{4,8},{8,12},{12,0},{1,5},{5,9},{9,13},{13,1},{2,6},{6,10},{... | collective-permute-start | bytes 1671176 | tf_op jit(solution)/shard_map/y3/ppermute | solution.py:431
  211.6 13.7 %copy-start.10 = (bf16[272,1024]{1,0:T(8,128)(2,1)}, bf16[272,1024]{1,0:T(8,128)(2,1)S(1)}, u32[]{:S(2)}) copy-start(bf16[272,1024]{1,0:T(8,128)(2,1)S(1)} %collective-permute-done.21.rest_7_.rest_11_) | copy-start | bytes 1671172
  (15 other events, 62.9 us)

commit v2 on v1

--- a/solution.py
+++ b/solution.py
@@ -351,7 +351,7 @@
 
 
 def finish_kernel(y_ref, mask_ref, mask0_ref, outer_ref, outer0_ref, inner_ref, *rest):
-    pieces, zeros, last, last0, (out_ref, held, held0) = rest[:2], rest[2:4], rest[4:8], rest[8:12], rest[12:]
+    pieces, zeros, last, last0, (out_ref, held, held0) = rest[:1], rest[1:2], rest[2:10], rest[10:18], rest[18:]
     step = pl.program_id(0)
     y = y_ref[0]
     lane_at = pl.multiple_of(step * 128, 128)
@@ -366,7 +366,7 @@
         both = outer0_ref[source, :, pl.ds(first_at, 128)].astype(jnp.float32)
         for pair in range(2):
             held0[pair, row, :] = both[pair * NF : (pair + 1) * NF]
-        for part in range(1, PARTS - 1):
+        for part in range(1, PARTS - 2):
             row = slice(source * 32 + part * NF, source * 32 + (part + 1) * NF)
             both = pieces[part - 1][source].astype(jnp.float32)
             for i in range(STEP):
@@ -374,8 +374,9 @@
             both = zeros[part - 1][source, :, pl.ds(lane_at, 128)].astype(jnp.float32)
             for pair in range(2):
                 held0[pair, row, :] = both[pair * NF : (pair + 1) * NF]
-    for s in range(4):
-        row = pl.ds(pl.multiple_of(lax.rem(y + 4 - s, 4) * 32 + (PARTS - 1) * NF, NF), NF)
+    for s in range(8):
+        part = PARTS - 2 + s // 4
+        row = pl.ds(pl.multiple_of(lax.rem(y + 4 - s % 4, 4) * 32 + part * NF, NF), NF)
         both = last[s][...].astype(jnp.float32)
         for i in range(STEP):
             held[i, row, :] = both[i * NF : (i + 1) * NF]
@@ -484,6 +485,11 @@
     def do_cross(part, visitors, after):
         return cross(tie(owns[part], after), (*visitors, swapped[part]))
 
+    def send_back(block, after, name):
+        sent = [lax.dynamic_index_in_dim(block, (y + s) % 4, 0, keepdims=False) for s in range(4)]
+        with jax.named_scope(name):
+            return [sent[0]] + [shift(tie(sent[s], after), "y", s) for s in range(1, 4)]
+
     owns = assemble(p0)
     swapped = [swap(0)]
     chosen = choose(0)
@@ -502,13 +508,11 @@
     y1 = exchange(tie(c1, y0), "y1")
     v2 = gather(2, choose(2), v0, c1)
     c2 = do_cross(2, v2, (c1, y0))
-    y2 = exchange(tie(c2, y1), "y2")
+    y2 = send_back(c2, None, "y2")
     v3 = gather(3, choose(3), v1, c2)
     c3 = do_cross(3, v3, (c2, y1))
-    y3 = [lax.dynamic_index_in_dim(c3, (y + s) % 4, 0, keepdims=False) for s in range(4)]
-    with jax.named_scope("y3"):
-        y3 = [y3[0]] + [shift(y3[s], "y", s) for s in range(1, 4)]
-    return finish(y_arg, mask, mask0, ya0, y0, (y1, y2), y3).reshape(32, 17, 32, 2, 128)
+    y3 = send_back(c3, None, "y3")
+    return finish(y_arg, mask, mask0, ya0, y0, (y1,), y2 + y3).reshape(32, 17, 32, 2, 128)
 
 
 def solution(mesh):

time: 238 us -> 233 us (0.979)
  waiting for transfers between devices: 89.2 us -> 82.2 us
  local copies, waits for them, and re-layouts: 11.9 us -> 14.8 us
    all_to_all x4 -> x3, waiting for transfers between devices: 11 us -> 6.17 us  [exchange(): return lax.all_to_all(block, 'y', 0, 0, tiled=True)]
    all_to_all x4 -> x3, starting transfers between devices: 17.3 us -> 12.8 us  [exchange(): return lax.all_to_all(block, 'y', 0, 0, tiled=True)]
    ppermute x19 -> x22, starting transfers between devices: 17.8 us -> 22.1 us  [shift(): lax.ppermute(block, axis, [(i, (i + distance) % size) for i in range(size)])]
    squeeze x1 -> x2, local copies, waits for them, and re-layouts: 2.6 us -> 5.59 us  [send_back(): lax.dynamic_index_in_dim(block, (y + s) % 4, 0, keepdims=False)]
    ppermute x19 -> x22, waiting for transfers between devices: 71.6 us -> 69.4 us  [shift(): lax.ppermute(block, axis, [(i, (i + distance) % size) for i in range(size)])]
  transfers between devices with their start and end apart: 28 -> 30, of which waited for: 13 -> 13; matrix products, arithmetic and copies ran while one was open for 5% -> 6% of each run, Pallas kernels for 15% -> 16%
where the time goes in v2:
time: 233 us; the launch traced here: 232 us
  waiting for transfers between devices  82.2 us (35%)
  Pallas kernels  55.9 us (24%)
  starting transfers between devices  53.4 us (23%)
  blocking collectives  17.7 us (8%)
  local copies, waits for them, and re-layouts  14.8 us (6%)
  other arithmetic  7.44 us (3%)
    ppermute x22, waiting for transfers between devices, shift(): lax.ppermute(block, axis, [(i, (i + distance) % size) for i in range(size)])  69.4 us
    ppermute x22, starting transfers between devices, shift(): lax.ppermute(block, axis, [(i, (i + distance) % size) for i in range(size)])  22.1 us
    pallas_call x3, Pallas kernels, cross(): pl.pallas_call(cross_kernel, grid=(1,), in_specs=[whole(NF, 128, 256) for...  18.9 us
    all_to_all x1, blocking collectives, transpose(): lax.all_to_all(tie(block, after), ('zh', 'core', 'y'), 0, 0, tiled=True)  17.7 us
    all_to_all x2, starting transfers between devices, transpose(): lax.all_to_all(tie(block, after), ('zh', 'core', 'y'), 0, 0, tiled=True)  13.1 us
    all_to_all x3, starting transfers between devices, exchange(): return lax.all_to_all(block, 'y', 0, 0, tiled=True)  12.8 us
    pallas_call x1, Pallas kernels, finish(): pl.pallas_call(finish_kernel, grid_spec=pltpu.PrefetchScalarGridSpec(num_...  10.7 us
    pallas_call x1, Pallas kernels, whiten(): pl.pallas_call(whiten_kernel, grid=(1024 // WROWS,), in_specs=[pl.BlockSp...  8.7 us
  transfers between devices with their start and end apart: 30, of which 13 were waited for; matrix products, arithmetic and copies ran while one was open for 6% of the time, Pallas kernels for 16%

profile of v2, /device:TPU:1, one launch (start us, length us, event | category | flops | bytes accessed | tf_op | source)
XLA Modules:
  0.0 231.9 jit_solution(9068979926793786512)
XLA Ops:
  1.3 5.0 %collective-permute-start.2 = (f32[8]{0:T(128)}, f32[8]{0:T(128)}, u32[]{:S(2)}, u32[]{:S(2)}) collective-permute-start(f32[8]{0:T(128)} %convert_reduce_fusion), channel_id=1, source_target_pairs={{0,3},{1,2},{2,1},{3,0},{4,7},{5,6},{6,5},{7,4},{8,11},{9,10},{10,... | collective-permute-start | bytes 104 | tf_op jit(solution)/shard_map/ppermute | solution.py:443
  11.2 4.6 %normalize.1.x_ref = bf16[1024,1024]{1,0:T(8,128)(2,1)S(1)} custom-call(bf16[1024,1024]{1,0:T(8,128)(2,1)S(1)} %bitcast.24, s32[32,4]{1,0:T(8,128)S(1)} %copy.28.starts_ref, s32[32,1]{1,0:T(8,128)S(1)} %copy.29.counts_ref, bf16[1024,1024]{1,0:T(8,128)(2,1)} %constant.104.clone.band_ref, f32[1,1024]{1,0:T(1,128)S(1)} %copy-done.5, f32[1,1024]{1,0:T(1,128)S(1)} %copy-done.4), custom_call_target="tpu_custom_call" | custom-call | flops 206999994368 | bytes 648000000 | tf_op jit(solution)/shard_map/normalize/pallas_call | solution.py:89
  16.7 8.7 %whiten.1 = (bf16[16,8,16,128]{3,2,1,0:T(8,128)(2,1)S(1)}, bf16[16,8,16,128]{3,2,1,0:T(8,128)(2,1)}, bf16[16,16,16,128]{3,2,1,0:T(8,128)(2,1)}) custom-call(bf16[1024,1024]{1,0:T(8,128)(2,1)S(1)} %normalize.1.x_ref, f32[1,1024]{1,0:T(1,128)S(1)} %broadcast_in_dim_reshape.3.root_ref, bf16[1024,1024]{1,0:T(8,128)(2,1)} %constant.107.clone.dft_ref, ...), custom_call_target="tpu_custom_call" | custom-call | flops 310499999744 | bytes 972000000 | tf_op jit(solution)/shard_map/whiten/pallas_call | solution.py:144
  25.4 17.7 %all_to_all.30.piece_ref = bf16[16,8,16,128]{3,2,1,0:T(8,128)(2,1)S(1)} all-to-all(bf16[16,8,16,128]{3,2,1,0:T(8,128)(2,1)S(1)} %get-tuple-element.39), channel_id=1, replica_groups=mesh['zl'=2,'x'=4,'y'=4,'zh'=2,'core'=2] {'zh','core','y'}, dimensions={0} | all-to-all | bytes 1048576 | tf_op jit(solution)/shard_map/p0/all_to_all | solution.py:463
  44.5 5.5 %all-to-all-start.1 = ((bf16[16,8,16,128]{3,2,1,0:T(8,128)(2,1)}), bf16[16,8,16,128]{3,2,1,0:T(8,128)(2,1)S(1)}, u32[]{:S(2)}, u32[]{:S(2)}) async-start(bf16[16,8,16,128]{3,2,1,0:T(8,128)(2,1)} %get-tuple-element.45), calls=%async_computation.1 | async-start | bytes 1048576 | tf_op jit(solution)/shard_map/p1/all_to_all | solution.py:463
  50.0 9.8 %collective-permute-done.3.v4_ref = bf16[8,128,256]{2,1,0:T(8,128)(2,1)S(1)} collective-permute-done((bf16[8,128,256]{2,1,0:T(8,128)(2,1)S(1)}, bf16[8,128,256]{2,1,0:T(8,128)(2,1)S(1)}, u32[]{:S(2)}, u32[]{:S(2)}) %collective-permute-start.3) | collective-permute-done | bytes 524320 | tf_op jit(solution)/shard_map/z0/ppermute | solution.py:432
  59.9 2.5 %collective-permute-start.4 = (bf16[8,128,256]{2,1,0:T(8,128)(2,1)S(1)}, bf16[8,128,256]{2,1,0:T(8,128)(2,1)}, u32[]{:S(2)}, u32[]{:S(2)}) collective-permute-start(bf16[8,128,256]{2,1,0:T(8,128)(2,1)S(1)} %get-tuple-element.40), channel_id=1, source_target_pairs={{0,48},{16,0},{32,16},{48,32},{1,49},{17,1},{33,17},{49,33},{2,50}... | collective-permute-start | bytes 1572872 | tf_op jit(solution)/shard_map/x0/ppermute | solution.py:432
  64.6 3.4 %outer.1 = bf16[4,320,256]{2,1,0:T(8,128)(2,1)} custom-call(bf16[8,128,256]{2,1,0:T(8,128)(2,1)} %copy-done, bf16[8,128,256]{2,1,0:T(8,128)(2,1)} %copy-done.8, bf16[256,512]{1,0:T(8,128)(2,1)} %constant.110.clone.spread_ref), custom_call_target="tpu_custom_call" | custom-call | flops 103499997184 | bytes 324000000 | tf_op jit(solution)/shard_map/outer/pallas_call | solution.py:320
  68.0 3.7 %all-to-all-start.2 = ((bf16[4,320,256]{2,1,0:T(8,128)(2,1)}), bf16[4,320,256]{2,1,0:T(8,128)(2,1)S(1)}, u32[]{:S(2)}, u32[]{:S(2)}) async-start(bf16[4,320,256]{2,1,0:T(8,128)(2,1)} %outer.1), calls=%async_computation.2 | async-start | bytes 1310720 | tf_op jit(solution)/shard_map/yA0/all_to_all | solution.py:475
  73.8 6.2 %all-to-all-done.2.outer_ref.outer0_ref = bf16[4,320,256]{2,1,0:T(8,128)(2,1)S(1)} async-done(((bf16[4,320,256]{2,1,0:T(8,128)(2,1)}), bf16[4,320,256]{2,1,0:T(8,128)(2,1)S(1)}, u32[]{:S(2)}, u32[]{:S(2)}) %all-to-all-start.2) | async-done | bytes 655392 | tf_op jit(solution)/shard_map/yA0/all_to_all | solution.py:475
  80.0 7.7 %all-to-all-start.3 = ((bf16[16,16,16,128]{3,2,1,0:T(8,128)(2,1)}), bf16[16,16,16,128]{3,2,1,0:T(8,128)(2,1)}, u32[]{:S(2)}, u32[]{:S(2)}) async-start(bf16[16,16,16,128]{3,2,1,0:T(8,128)(2,1)} %get-tuple-element.48), calls=%async_computation.3 | async-start | bytes 2097152 | tf_op jit(solution)/shard_map/p23/all_to_all | solution.py:463
  89.1 4.8 %inner.1 = bf16[4,256,768]{2,1,0:T(8,128)(2,1)} custom-call(bf16[8,128,256]{2,1,0:T(8,128)(2,1)} %copy-done, bf16[8,128,256]{2,1,0:T(8,128)(2,1)} %collective-permute-done.4.v1_ref, bf16[8,128,256]{2,1,0:T(8,128)(2,1)} %collective-permute-done.5.v2_ref, bf16[8,128,256]{2,1,0:T(8,128)(2,1)} %collective-permute-done.6.v3_ref, ...), custom_call_target="tpu_custom_call" | custom-call | flops 172499992576 | bytes 540000000 | tf_op jit(solution)/shard_map/inner/pallas_call | solution.py:320
  97.8 5.5 %all-to-all-done.3.piece_ref = bf16[16,16,16,128]{3,2,1,0:T(8,128)(2,1)} async-done(((bf16[16,16,16,128]{3,2,1,0:T(8,128)(2,1)}), bf16[16,16,16,128]{3,2,1,0:T(8,128)(2,1)}, u32[]{:S(2)}, u32[]{:S(2)}) %all-to-all-start.3) | async-done | bytes 1048608 | tf_op jit(solution)/shard_map/p23/all_to_all | solution.py:463
  103.3 3.0 %assemble.5 = (bf16[8,128,256]{2,1,0:T(8,128)(2,1)}, bf16[8,128,256]{2,1,0:T(8,128)(2,1)}) custom-call(bf16[16,16,16,128]{3,2,1,0:T(8,128)(2,1)} %all-to-all-done.3.piece_ref), custom_call_target="tpu_custom_call" | custom-call | flops 55199997952 | bytes 172800000 | tf_op jit(solution)/shard_map/assemble/pallas_call | solution.py:200
  107.8 4.4 %all-to-all-start.4 = ((bf16[4,256,768]{2,1,0:T(8,128)(2,1)}), bf16[4,256,768]{2,1,0:T(8,128)(2,1)}, u32[]{:S(2)}, u32[]{:S(2)}) async-start(bf16[4,256,768]{2,1,0:T(8,128)(2,1)} %inner.1), calls=%async_computation.4 | async-start | bytes 3145728 | tf_op jit(solution)/shard_map/y0/all_to_all | solution.py:475
  112.1 7.5 %collective-permute-done.8.v1_ref = bf16[8,128,256]{2,1,0:T(8,128)(2,1)S(1)} collective-permute-done((bf16[8,128,256]{2,1,0:T(8,128)(2,1)S(1)}, bf16[8,128,256]{2,1,0:T(8,128)(2,1)S(1)}, u32[]{:S(2)}, u32[]{:S(2)}) %collective-permute-start.8) | collective-permute-done | bytes 524320 | tf_op jit(solution)/shard_map/x1/ppermute | solution.py:432
  119.6 2.3 %collective-permute-done.10.v3_ref = bf16[8,128,256]{2,1,0:T(8,128)(2,1)S(1)} collective-permute-done((bf16[8,128,256]{2,1,0:T(8,128)(2,1)S(1)}, bf16[8,128,256]{2,1,0:T(8,128)(2,1)S(1)}, u32[]{:S(2)}, u32[]{:S(2)}) %collective-permute-start.10) | collective-permute-done | bytes 524320 | tf_op jit(solution)/shard_map/x1/ppermute | solution.py:432
  122.8 6.3 %cross.3 = bf16[4,272,1024]{2,1,0:T(8,128)(2,1)} custom-call(bf16[8,128,256]{2,1,0:T(8,128)(2,1)} %assemble.4.own_ref, bf16[8,128,256]{2,1,0:T(8,128)(2,1)} %copy-done.16, bf16[8,128,256]{2,1,0:T(8,128)(2,1)} %copy-done.14, bf16[8,128,256]{2,1,0:T(8,128)(2,1)} %copy-done.17, bf16[8,128,256]{2,1,0:T(8,128)(2,1)} %collective-permute-done.7.v4_ref, ...), custom_call_target="tpu_custom_call" | custom-call | flops 344999985152 | bytes 1080000000 | tf_op jit(solution)/shard_map/cross/pallas_call | solution.py:256
  133.2 2.5 %broadcast_select_fusion = (bf16[8,128,256]{2,1,0:T(8,128)(2,1)}, bf16[8,128,256]{2,1,0:T(8,128)(2,1)}, bf16[8,128,256]{2,1,0:T(8,128)(2,1)}) fusion(bf16[8,128,256]{2,1,0:T(8,128)(2,1)} %collective-permute-done.18.v4_ref, bf16[8,128,256]{2,1,0:T(8,128)(2,1)} %get-tuple-element.66.own_ref, pred[]{:T(512)S(6)} %lt.77, pred[]{:T(512)S(6)} %lt.76, pred[]{:T(512)S(6)} %lt.75), kind=kLoop, calls=%fused_computation.11 | loop fusion | flops 786432 | bytes 2621443 | tf_op jit(solution)/shard_map/x3/jit(_where)/select_n | solution.py:479
  137.3 4.7 %all-to-all-start.5 = ((bf16[4,272,1024]{2,1,0:T(8,128)(2,1)}), bf16[4,272,1024]{2,1,0:T(8,128)(2,1)}, u32[]{:S(2)}, u32[]{:S(2)}) async-start(bf16[4,272,1024]{2,1,0:T(8,128)(2,1)} %cross.3), calls=%async_computation.5 | async-start | bytes 4456448 | tf_op jit(solution)/shard_map/y1/all_to_all | solution.py:475
  142.0 2.8 %collective-permute-done.14.v3_ref = bf16[8,128,256]{2,1,0:T(8,128)(2,1)S(1)} collective-permute-done((bf16[8,128,256]{2,1,0:T(8,128)(2,1)S(1)}, bf16[8,128,256]{2,1,0:T(8,128)(2,1)S(1)}, u32[]{:S(2)}, u32[]{:S(2)}) %collective-permute-start.14) | collective-permute-done | bytes 524320 | tf_op jit(solution)/shard_map/x2/ppermute | solution.py:432
  144.8 11.4 %collective-permute-done.13.v2_ref = bf16[8,128,256]{2,1,0:T(8,128)(2,1)S(1)} collective-permute-done((bf16[8,128,256]{2,1,0:T(8,128)(2,1)S(1)}, bf16[8,128,256]{2,1,0:T(8,128)(2,1)S(1)}, u32[]{:S(2)}, u32[]{:S(2)}) %collective-permute-start.13) | collective-permute-done | bytes 524320 | tf_op jit(solution)/shard_map/x2/ppermute | solution.py:432
  157.0 6.4 %cross.4 = bf16[4,272,1024]{2,1,0:T(8,128)(2,1)} custom-call(bf16[8,128,256]{2,1,0:T(8,128)(2,1)} %get-tuple-element.59.own_ref, bf16[8,128,256]{2,1,0:T(8,128)(2,1)} %copy-done.13, bf16[8,128,256]{2,1,0:T(8,128)(2,1)} %copy-done.15, bf16[8,128,256]{2,1,0:T(8,128)(2,1)} %copy-done.12, bf16[8,128,256]{2,1,0:T(8,128)(2,1)} %collective-permute-done.11.v4_ref, ...), custom_call_target="tpu_custom_call" | custom-call | flops 344999985152 | bytes 1080000000 | tf_op jit(solution)/shard_map/cross/pallas_call | solution.py:256
  163.9 3.0 %dynamic-slice_bitcast_fusion.4 = (bf16[272,1024]{1,0:T(8,128)(2,1)}, bf16[272,1024]{1,0:T(8,128)(2,1)}, bf16[272,1024]{1,0:T(8,128)(2,1)}, bf16[272,1024]{1,0:T(8,128)(2,1)}) fusion(bf16[4,272,1024]{2,1,0:T(8,128)(2,1)} %cross.4, s32[]{:T(128)S(6)} %select_n.133, s32[]{:T(128)S(6)} %select_n.131, s32[]{:T(128)S(6)} %select_n.129, s32[]{:T(128)S(6)} %select_n.127), kind=kLoop, calls=%fused_computation.6 | loop fusion | bytes 4456464 | tf_op jit(solution)/shard_map/jit(dynamic_index_in_dim)/squeeze | solution.py:489
  166.9 2.6 %collective-permute-start.17 = (bf16[272,1024]{1,0:T(8,128)(2,1)}, bf16[272,1024]{1,0:T(8,128)(2,1)}, u32[]{:S(2)}, u32[]{:S(2)}) collective-permute-start(bf16[272,1024]{1,0:T(8,128)(2,1)} %get-tuple-element.77), channel_id=1, source_target_pairs={{0,12},{4,0},{8,4},{12,8},{1,13},{5,1},{9,5},{13,9},{2,14},{6,2},{... | collective-permute-start | bytes 1671176 | tf_op jit(solution)/shard_map/y2/ppermute | solution.py:432
  171.2 5.7 %collective-permute-done.20.v2_ref = bf16[8,128,256]{2,1,0:T(8,128)(2,1)S(1)} collective-permute-done((bf16[8,128,256]{2,1,0:T(8,128)(2,1)S(1)}, bf16[8,128,256]{2,1,0:T(8,128)(2,1)S(1)}, u32[]{:S(2)}, u32[]{:S(2)}) %collective-permute-start.20) | collective-permute-done | bytes 524320 | tf_op jit(solution)/shard_map/x3/ppermute | solution.py:432
  177.7 6.3 %cross.5 = bf16[4,272,1024]{2,1,0:T(8,128)(2,1)} custom-call(bf16[8,128,256]{2,1,0:T(8,128)(2,1)} %get-tuple-element.66.own_ref, bf16[8,128,256]{2,1,0:T(8,128)(2,1)} %collective-permute-done.19.v1_ref, bf16[8,128,256]{2,1,0:T(8,128)(2,1)} %copy-done.11, bf16[8,128,256]{2,1,0:T(8,128)(2,1)} %collective-permute-done.21.v3_ref, ...), custom_call_target="tpu_custom_call" | custom-call | flops 344999985152 | bytes 1080000000 | tf_op jit(solution)/shard_map/cross/pallas_call | solution.py:256
  184.0 2.6 %dynamic-slice_bitcast_fusion = (bf16[272,1024]{1,0:T(8,128)(2,1)S(1)}, bf16[272,1024]{1,0:T(8,128)(2,1)S(1)}, bf16[272,1024]{1,0:T(8,128)(2,1)S(1)}, bf16[272,1024]{1,0:T(8,128)(2,1)}) fusion(bf16[4,272,1024]{2,1,0:T(8,128)(2,1)} %cross.5, s32[]{:T(128)S(6)} %select_n.133, s32[]{:T(128)S(6)} %select_n.131, s32[]{:T(128)S(6)} %select_n.129, s32[]{:T(128)S(6)} %select_n.127), kind=kLoop, calls=%fused_computation.2 | loop fusion | bytes 4456464 | tf_op jit(solution)/shard_map/jit(dynamic_index_in_dim)/squeeze | solution.py:489
  192.5 7.4 %collective-permute-done.15.rest_3_.rest_11_ = bf16[272,1024]{1,0:T(8,128)(2,1)} collective-permute-done((bf16[272,1024]{1,0:T(8,128)(2,1)}, bf16[272,1024]{1,0:T(8,128)(2,1)}, u32[]{:S(2)}, u32[]{:S(2)}) %collective-permute-start.15) | collective-permute-done | bytes 557088 | tf_op jit(solution)/shard_map/y2/ppermute | solution.py:432
  199.9 7.8 %collective-permute-done.24.rest_9_.rest_17_ = bf16[272,1024]{1,0:T(8,128)(2,1)S(1)} collective-permute-done((bf16[272,1024]{1,0:T(8,128)(2,1)S(1)}, bf16[272,1024]{1,0:T(8,128)(2,1)S(1)}, u32[]{:S(2)}, u32[]{:S(2)}) %collective-permute-start.24) | collective-permute-done | bytes 557088 | tf_op jit(solution)/shard_map/y3/ppermute | solution.py:432
  207.6 13.4 %collective-permute-done.22.rest_7_.rest_15_ = bf16[272,1024]{1,0:T(8,128)(2,1)} collective-permute-done((bf16[272,1024]{1,0:T(8,128)(2,1)S(1)}, bf16[272,1024]{1,0:T(8,128)(2,1)}, u32[]{:S(2)}, u32[]{:S(2)}) %collective-permute-start.22) | collective-permute-done | bytes 557088 | tf_op jit(solution)/shard_map/y3/ppermute | solution.py:432
  221.1 10.7 %finish.1 = bf16[34816,128]{1,0:T(8,128)(2,1)} custom-call(s32[1]{0:T(128)} %bitcast.y_ref, f32[8,4,1024]{2,1,0:T(4,128)} %reshape.14.mask_ref, f32[16,1,128]{2,1,0:T(1,128)} %reshape_squeeze.3.mask0_ref, bf16[4,320,256]{2,1,0:T(8,128)(2,1)} %copy-done.6, bf16[4,320,256]{2,1,0:T(8,128)(2,1)} %copy-done.6, bf16[4,256,768]{2,1,0:T(8,128)(2,1)} %all-to-all-done.4.inner_ref, ...), custom_call_target="tpu_custom_call" | custom-call | flops 310499999744 | bytes 972000000 | tf_op jit(solution)/shard_map/finish/pallas_call | solution.py:399
  (102 shorter events, 35.9 us)
Async XLA Ops:
  1.3 14.5 %collective-permute-start.2 = (f32[8]{0:T(128)}, f32[8]{0:T(128)}, u32[]{:S(2)}, u32[]{:S(2)}) collective-permute-start(f32[8]{0:T(128)} %convert_reduce_fusion), channel_id=1, source_target_pairs={{0,3},{1,2},{2,1},{3,0},{4,7},{5,6},{6,5},{7,4},{8,11},{9,10},{10,... | collective-permute-start | bytes 104 | tf_op jit(solution)/shard_map/ppermute | solution.py:443
  6.3 9.5 %collective-permute-start.1 = (f32[8]{0:T(128)}, f32[8]{0:T(128)}, u32[]{:S(2)}, u32[]{:S(2)}) collective-permute-start(f32[8]{0:T(128)} %convert_reduce_fusion), channel_id=1, source_target_pairs={{0,2},{1,3},{2,0},{3,1},{4,6},{5,7},{6,4},{7,5},{8,10},{9,11},{10,... | collective-permute-start | bytes 104 | tf_op jit(solution)/shard_map/ppermute | solution.py:443
  6.3 9.5 %collective-permute-start = (f32[8]{0:T(128)}, f32[8]{0:T(128)}, u32[]{:S(2)}, u32[]{:S(2)}) collective-permute-start(f32[8]{0:T(128)} %convert_reduce_fusion), channel_id=1, source_target_pairs={{0,1},{1,0},{2,3},{3,2},{4,5},{5,4},{6,7},{7,6},{8,9},{9,8},{10,11... | collective-permute-start | bytes 104 | tf_op jit(solution)/shard_map/ppermute | solution.py:443
  43.7 21.0 %copy-start = (bf16[8,128,256]{2,1,0:T(8,128)(2,1)}, bf16[8,128,256]{2,1,0:T(8,128)(2,1)S(1)}, u32[]{:S(2)}) copy-start(bf16[8,128,256]{2,1,0:T(8,128)(2,1)S(1)} %assemble.3.own_ref) | copy-start | bytes 1572868
  43.7 16.1 %collective-permute-start.3 = (bf16[8,128,256]{2,1,0:T(8,128)(2,1)S(1)}, bf16[8,128,256]{2,1,0:T(8,128)(2,1)S(1)}, u32[]{:S(2)}, u32[]{:S(2)}) collective-permute-start(bf16[8,128,256]{2,1,0:T(8,128)(2,1)S(1)} %assemble.3.own_ref), channel_id=1, source_target_pairs={{0,64},{64,0},{1,65},{65,1},{2,66},{66,2},{3,67},{67,3},{4,68},{68... | collective-permute-start | bytes 1572872 | tf_op jit(solution)/shard_map/z0/ppermute | solution.py:432
  44.5 20.1 %all-to-all-start.1 = ((bf16[16,8,16,128]{3,2,1,0:T(8,128)(2,1)}), bf16[16,8,16,128]{3,2,1,0:T(8,128)(2,1)S(1)}, u32[]{:S(2)}, u32[]{:S(2)}) async-start(bf16[16,8,16,128]{3,2,1,0:T(8,128)(2,1)} %get-tuple-element.45), calls=%async_computation.1 | async-start | bytes 1048576 | tf_op jit(solution)/shard_map/p1/all_to_all | solution.py:463
  59.9 27.8 %collective-permute-start.4 = (bf16[8,128,256]{2,1,0:T(8,128)(2,1)S(1)}, bf16[8,128,256]{2,1,0:T(8,128)(2,1)}, u32[]{:S(2)}, u32[]{:S(2)}) collective-permute-start(bf16[8,128,256]{2,1,0:T(8,128)(2,1)S(1)} %get-tuple-element.40), channel_id=1, source_target_pairs={{0,48},{16,0},{32,16},{48,32},{1,49},{17,1},{33,17},{49,33},{2,50}... | collective-permute-start | bytes 1572872 | tf_op jit(solution)/shard_map/x0/ppermute | solution.py:432
  62.4 25.3 %collective-permute-start.5 = (bf16[8,128,256]{2,1,0:T(8,128)(2,1)S(1)}, bf16[8,128,256]{2,1,0:T(8,128)(2,1)}, u32[]{:S(2)}, u32[]{:S(2)}) collective-permute-start(bf16[8,128,256]{2,1,0:T(8,128)(2,1)S(1)} %get-tuple-element.41), channel_id=1, source_target_pairs={{0,32},{16,48},{32,0},{48,16},{1,33},{17,49},{33,1},{49,17},{2,34}... | collective-permute-start | bytes 1572872 | tf_op jit(solution)/shard_map/x0/ppermute | solution.py:432
  63.0 26.1 %collective-permute-start.6 = (bf16[8,128,256]{2,1,0:T(8,128)(2,1)S(1)}, bf16[8,128,256]{2,1,0:T(8,128)(2,1)}, u32[]{:S(2)}, u32[]{:S(2)}) collective-permute-start(bf16[8,128,256]{2,1,0:T(8,128)(2,1)S(1)} %get-tuple-element.42), channel_id=1, source_target_pairs={{0,16},{16,32},{32,48},{48,0},{1,17},{17,33},{33,49},{49,1},{2,18}... | collective-permute-start | bytes 1572872 | tf_op jit(solution)/shard_map/x0/ppermute | solution.py:432
  68.0 12.0 %all-to-all-start.2 = ((bf16[4,320,256]{2,1,0:T(8,128)(2,1)}), bf16[4,320,256]{2,1,0:T(8,128)(2,1)S(1)}, u32[]{:S(2)}, u32[]{:S(2)}) async-start(bf16[4,320,256]{2,1,0:T(8,128)(2,1)} %outer.1), calls=%async_computation.2 | async-start | bytes 1310720 | tf_op jit(solution)/shard_map/yA0/all_to_all | solution.py:475
  73.1 20.8 %collective-permute-start.7 = (bf16[8,128,256]{2,1,0:T(8,128)(2,1)}, bf16[8,128,256]{2,1,0:T(8,128)(2,1)}, u32[]{:S(2)}, u32[]{:S(2)}) collective-permute-start(bf16[8,128,256]{2,1,0:T(8,128)(2,1)} %assemble.4.own_ref), channel_id=1, source_target_pairs={{0,64},{64,0},{1,65},{65,1},{2,66},{66,2},{3,67},{67,3},{4,68},{68... | collective-permute-start | bytes 1572872 | tf_op jit(solution)/shard_map/z1/ppermute | solution.py:432
  80.0 13.9 %copy-start.6 = (bf16[4,320,256]{2,1,0:T(8,128)(2,1)}, bf16[4,320,256]{2,1,0:T(8,128)(2,1)S(1)}, u32[]{:S(2)}) copy-start(bf16[4,320,256]{2,1,0:T(8,128)(2,1)S(1)} %all-to-all-done.2.outer_ref.outer0_ref) | copy-start | bytes 1966084
  80.0 23.3 %all-to-all-start.3 = ((bf16[16,16,16,128]{3,2,1,0:T(8,128)(2,1)}), bf16[16,16,16,128]{3,2,1,0:T(8,128)(2,1)}, u32[]{:S(2)}, u32[]{:S(2)}) async-start(bf16[16,16,16,128]{3,2,1,0:T(8,128)(2,1)} %get-tuple-element.48), calls=%async_computation.3 | async-start | bytes 2097152 | tf_op jit(solution)/shard_map/p23/all_to_all | solution.py:463
  95.2 16.9 %collective-permute-start.9 = (bf16[8,128,256]{2,1,0:T(8,128)(2,1)S(1)}, bf16[8,128,256]{2,1,0:T(8,128)(2,1)S(1)}, u32[]{:S(2)}, u32[]{:S(2)}) collective-permute-start(bf16[8,128,256]{2,1,0:T(8,128)(2,1)S(1)} %get-tuple-element.56), channel_id=1, source_target_pairs={{0,32},{16,48},{32,0},{48,16},{1,33},{17,49},{33,1},{49,17},{2,34}... | collective-permute-start | bytes 1572872 | tf_op jit(solution)/shard_map/x1/ppermute | solution.py:432
  96.3 23.3 %collective-permute-start.8 = (bf16[8,128,256]{2,1,0:T(8,128)(2,1)S(1)}, bf16[8,128,256]{2,1,0:T(8,128)(2,1)S(1)}, u32[]{:S(2)}, u32[]{:S(2)}) collective-permute-start(bf16[8,128,256]{2,1,0:T(8,128)(2,1)S(1)} %get-tuple-element.54), channel_id=1, source_target_pairs={{0,48},{16,0},{32,16},{48,32},{1,49},{17,1},{33,17},{49,33},{2,50}... | collective-permute-start | bytes 1572872 | tf_op jit(solution)/shard_map/x1/ppermute | solution.py:432
  97.8 24.2 %collective-permute-start.10 = (bf16[8,128,256]{2,1,0:T(8,128)(2,1)S(1)}, bf16[8,128,256]{2,1,0:T(8,128)(2,1)S(1)}, u32[]{:S(2)}, u32[]{:S(2)}) collective-permute-start(bf16[8,128,256]{2,1,0:T(8,128)(2,1)S(1)} %get-tuple-element.57), channel_id=1, source_target_pairs={{0,16},{16,32},{32,48},{48,0},{1,17},{17,33},{33,49},{49,1},{2,18}... | collective-permute-start | bytes 1572872 | tf_op jit(solution)/shard_map/x1/ppermute | solution.py:432
  106.3 22.8 %collective-permute-start.11 = (bf16[8,128,256]{2,1,0:T(8,128)(2,1)}, bf16[8,128,256]{2,1,0:T(8,128)(2,1)}, u32[]{:S(2)}, u32[]{:S(2)}) collective-permute-start(bf16[8,128,256]{2,1,0:T(8,128)(2,1)} %get-tuple-element.59.own_ref), channel_id=1, source_target_pairs={{0,64},{64,0},{1,65},{65,1},{2,66},{66,2},{3,67},{67,3},{4,68},{68... | collective-permute-start | bytes 1572872 | tf_op jit(solution)/shard_map/z2/ppermute | solution.py:432
  107.1 26.2 %collective-permute-start.18 = (bf16[8,128,256]{2,1,0:T(8,128)(2,1)}, bf16[8,128,256]{2,1,0:T(8,128)(2,1)}, u32[]{:S(2)}, u32[]{:S(2)}) collective-permute-start(bf16[8,128,256]{2,1,0:T(8,128)(2,1)} %get-tuple-element.66.own_ref), channel_id=1, source_target_pairs={{0,64},{64,0},{1,65},{65,1},{2,66},{66,2},{3,67},{67,3},{4,68},{68... | collective-permute-start | bytes 1572872 | tf_op jit(solution)/shard_map/z3/ppermute | solution.py:432
  107.8 29.5 %all-to-all-start.4 = ((bf16[4,256,768]{2,1,0:T(8,128)(2,1)}), bf16[4,256,768]{2,1,0:T(8,128)(2,1)}, u32[]{:S(2)}, u32[]{:S(2)}) async-start(bf16[4,256,768]{2,1,0:T(8,128)(2,1)} %inner.1), calls=%async_computation.4 | async-start | bytes 3145728 | tf_op jit(solution)/shard_map/y0/all_to_all | solution.py:475
  130.4 14.4 %collective-permute-start.14 = (bf16[8,128,256]{2,1,0:T(8,128)(2,1)S(1)}, bf16[8,128,256]{2,1,0:T(8,128)(2,1)S(1)}, u32[]{:S(2)}, u32[]{:S(2)}) collective-permute-start(bf16[8,128,256]{2,1,0:T(8,128)(2,1)S(1)} %get-tuple-element.65), channel_id=1, source_target_pairs={{0,16},{16,32},{32,48},{48,0},{1,17},{17,33},{33,49},{49,1},{2,18}... | collective-permute-start | bytes 1572872 | tf_op jit(solution)/shard_map/x2/ppermute | solution.py:432
  130.9 13.9 %collective-permute-start.12 = (bf16[8,128,256]{2,1,0:T(8,128)(2,1)S(1)}, bf16[8,128,256]{2,1,0:T(8,128)(2,1)S(1)}, u32[]{:S(2)}, u32[]{:S(2)}) collective-permute-start(bf16[8,128,256]{2,1,0:T(8,128)(2,1)S(1)} %get-tuple-element.61), channel_id=1, source_target_pairs={{0,48},{16,0},{32,16},{48,32},{1,49},{17,1},{33,17},{49,33},{2,50}... | collective-permute-start | bytes 1572872 | tf_op jit(solution)/shard_map/x2/ppermute | solution.py:432
  133.1 23.0 %collective-permute-start.13 = (bf16[8,128,256]{2,1,0:T(8,128)(2,1)S(1)}, bf16[8,128,256]{2,1,0:T(8,128)(2,1)S(1)}, u32[]{:S(2)}, u32[]{:S(2)}) collective-permute-start(bf16[8,128,256]{2,1,0:T(8,128)(2,1)S(1)} %get-tuple-element.63), channel_id=1, source_target_pairs={{0,32},{16,48},{32,0},{48,16},{1,33},{17,49},{33,1},{49,17},{2,34}... | collective-permute-start | bytes 1572872 | tf_op jit(solution)/shard_map/x2/ppermute | solution.py:432
  135.8 34.6 %collective-permute-start.19 = (bf16[8,128,256]{2,1,0:T(8,128)(2,1)}, bf16[8,128,256]{2,1,0:T(8,128)(2,1)}, u32[]{:S(2)}, u32[]{:S(2)}) collective-permute-start(bf16[8,128,256]{2,1,0:T(8,128)(2,1)} %get-tuple-element.68), channel_id=1, source_target_pairs={{0,48},{16,0},{32,16},{48,32},{1,49},{17,1},{33,17},{49,33},{2,50}... | collective-permute-start | bytes 1572872 | tf_op jit(solution)/shard_map/x3/ppermute | solution.py:432
  137.3 34.0 %collective-permute-start.21 = (bf16[8,128,256]{2,1,0:T(8,128)(2,1)}, bf16[8,128,256]{2,1,0:T(8,128)(2,1)}, u32[]{:S(2)}, u32[]{:S(2)}) collective-permute-start(bf16[8,128,256]{2,1,0:T(8,128)(2,1)} %get-tuple-element.72), channel_id=1, source_target_pairs={{0,16},{16,32},{32,48},{48,0},{1,17},{17,33},{33,49},{49,1},{2,18}... | collective-permute-start | bytes 1572872 | tf_op jit(solution)/shard_map/x3/ppermute | solution.py:432
  137.3 33.1 %all-to-all-start.5 = ((bf16[4,272,1024]{2,1,0:T(8,128)(2,1)}), bf16[4,272,1024]{2,1,0:T(8,128)(2,1)}, u32[]{:S(2)}, u32[]{:S(2)}) async-start(bf16[4,272,1024]{2,1,0:T(8,128)(2,1)} %cross.3), calls=%async_computation.5 | async-start | bytes 4456448 | tf_op jit(solution)/shard_map/y1/all_to_all | solution.py:475
  163.4 13.5 %collective-permute-start.20 = (bf16[8,128,256]{2,1,0:T(8,128)(2,1)S(1)}, bf16[8,128,256]{2,1,0:T(8,128)(2,1)S(1)}, u32[]{:S(2)}, u32[]{:S(2)}) collective-permute-start(bf16[8,128,256]{2,1,0:T(8,128)(2,1)S(1)} %copy-done.7), channel_id=1, source_target_pairs={{0,32},{16,48},{32,0},{48,16},{1,33},{17,49},{33,1},{49,17},{2,34}... | collective-permute-start | bytes 1572872 | tf_op jit(solution)/shard_map/x3/ppermute | solution.py:432
  166.9 23.2 %collective-permute-start.17 = (bf16[272,1024]{1,0:T(8,128)(2,1)}, bf16[272,1024]{1,0:T(8,128)(2,1)}, u32[]{:S(2)}, u32[]{:S(2)}) collective-permute-start(bf16[272,1024]{1,0:T(8,128)(2,1)} %get-tuple-element.77), channel_id=1, source_target_pairs={{0,12},{4,0},{8,4},{12,8},{1,13},{5,1},{9,5},{13,9},{2,14},{6,2},{... | collective-permute-start | bytes 1671176 | tf_op jit(solution)/shard_map/y2/ppermute | solution.py:432
  169.5 23.0 %collective-permute-start.16 = (bf16[272,1024]{1,0:T(8,128)(2,1)}, bf16[272,1024]{1,0:T(8,128)(2,1)}, u32[]{:S(2)}, u32[]{:S(2)}) collective-permute-start(bf16[272,1024]{1,0:T(8,128)(2,1)} %get-tuple-element.78), channel_id=1, source_target_pairs={{0,8},{4,12},{8,0},{12,4},{1,9},{5,13},{9,1},{13,5},{2,10},{6,14},... | collective-permute-start | bytes 1671176 | tf_op jit(solution)/shard_map/y2/ppermute | solution.py:432
  170.4 29.5 %collective-permute-start.15 = (bf16[272,1024]{1,0:T(8,128)(2,1)}, bf16[272,1024]{1,0:T(8,128)(2,1)}, u32[]{:S(2)}, u32[]{:S(2)}) collective-permute-start(bf16[272,1024]{1,0:T(8,128)(2,1)} %get-tuple-element.79), channel_id=1, source_target_pairs={{0,4},{4,8},{8,12},{12,0},{1,5},{5,9},{9,13},{13,1},{2,6},{6,10},{... | collective-permute-start | bytes 1671176 | tf_op jit(solution)/shard_map/y2/ppermute | solution.py:432
  186.5 21.1 %collective-permute-start.24 = (bf16[272,1024]{1,0:T(8,128)(2,1)S(1)}, bf16[272,1024]{1,0:T(8,128)(2,1)S(1)}, u32[]{:S(2)}, u32[]{:S(2)}) collective-permute-start(bf16[272,1024]{1,0:T(8,128)(2,1)S(1)} %get-tuple-element.73), channel_id=1, source_target_pairs={{0,12},{4,0},{8,4},{12,8},{1,13},{5,1},{9,5},{13,9},{2,14},{6,2},{... | collective-permute-start | bytes 1671176 | tf_op jit(solution)/shard_map/y3/ppermute | solution.py:432
  188.8 18.9 %collective-permute-start.23 = (bf16[272,1024]{1,0:T(8,128)(2,1)S(1)}, bf16[272,1024]{1,0:T(8,128)(2,1)}, u32[]{:S(2)}, u32[]{:S(2)}) collective-permute-start(bf16[272,1024]{1,0:T(8,128)(2,1)S(1)} %get-tuple-element.74), channel_id=1, source_target_pairs={{0,8},{4,12},{8,0},{12,4},{1,9},{5,13},{9,1},{13,5},{2,10},{6,14},... | collective-permute-start | bytes 1671176 | tf_op jit(solution)/shard_map/y3/ppermute | solution.py:432
  190.1 30.9 %collective-permute-start.22 = (bf16[272,1024]{1,0:T(8,128)(2,1)S(1)}, bf16[272,1024]{1,0:T(8,128)(2,1)}, u32[]{:S(2)}, u32[]{:S(2)}) collective-permute-start(bf16[272,1024]{1,0:T(8,128)(2,1)S(1)} %get-tuple-element.75), channel_id=1, source_target_pairs={{0,4},{4,8},{8,12},{12,0},{1,5},{5,9},{9,13},{13,1},{2,6},{6,10},{... | collective-permute-start | bytes 1671176 | tf_op jit(solution)/shard_map/y3/ppermute | solution.py:432
  (17 other events, 87.6 us)
